TPU v7x, 32 devices: a whole 2x2x4 slice. The times are simulated.
32 devices in a mesh: aux: 2 (over core), row: 4 (over z), col: 4 (over y, x).
Axes of the slice: x: 2, y: 2, z: 4, core: 2. Of those that a mesh axis runs over, the one named last changes fastest.
Arguments:
- coulomb: bfloat16 [64, 2048, 2048], P('aux', 'row', 'col'), may hold values from -6 to 6
- occupied: bfloat16 [2048, 2048], P('row'), may hold values from -0.125 to 0.125
- virtual: bfloat16 [2048, 2048], P('row'), may hold values from -0.125 to 0.125
- tile_mask: int32 [16, 16], replicated, may hold values 0 or 1
Outputs:
- chi: float32 [64, 64], P('aux')
All inputs are finite; a program needn't handle non-finite values.
Results may differ from a plain program's by a relative error of at most 0.0042.
Values may be sent and summed in bfloat16 or wider, within the bound.
No kernel may reach another device: no remote copies, remote signals or barrier semaphores. Data moves between devices by JAX's collectives and lax.ppermute only.
A program may use at most 192 MiB of HBM per device.

v0:
```python
import jax
import jax.numpy as jnp
from jax import lax
from jax.experimental import pallas as pl
from jax.experimental.pallas import tpu as pltpu
from jax.sharding import PartitionSpec as P

NAO = 2048
TILE = 128
VMEM_BYTES = 48 * 2**20
F32 = jnp.float32
BF16 = jnp.bfloat16
ANY = pl.BlockSpec(memory_space=pl.ANY)
WHOLE = pl.BlockSpec(memory_space=pltpu.VMEM)


def swapped(value, axis, apart):
    if apart == 0:
        return value
    pairs = [(source, source ^ apart) for source in range(lax.axis_size(axis))]
    return lax.ppermute(value, axis, pairs)


def cost(flops, moved):
    return pl.CostEstimate(flops=flops, bytes_accessed=moved, transcendentals=0)


def params():
    return pltpu.CompilerParams(vmem_limit_bytes=VMEM_BYTES)


def ordered(value, after):
    def body(*refs):
        del refs

    return pl.pallas_call(
        body,
        in_specs=[ANY] * (1 + len(after)),
        out_specs=ANY,
        out_shape=jax.ShapeDtypeStruct(value.shape, value.dtype),
        input_output_aliases={0: 0},
        name="ordered",
    )(value, *after)


def own_parts(blocks, place, part, after):
    count, nao = len(blocks), blocks[0].shape[1]

    def body(place_ref, *refs):
        for index in range(count):
            refs[count + len(after)][index] = refs[index][...]

    return pl.pallas_call(
        body,
        grid_spec=pltpu.PrefetchScalarGridSpec(
            num_scalar_prefetch=1,
            grid=(1,),
            in_specs=[pl.BlockSpec((part, nao), lambda i, place: (place[0], 0))] * count
            + [ANY] * len(after),
            out_specs=pl.BlockSpec((count, part, nao), lambda i, place: (0, 0, 0)),
        ),
        out_shape=jax.ShapeDtypeStruct((count, part, nao), BF16),
        name="own_parts",
    )(place.reshape(1), *blocks, *after)


def masked_piece(by_source, tiles, first, per, after):
    rows, _, mrow, ncol = by_source.shape

    def body(tiles_ref, source, *refs):
        target = refs[len(after)]
        for down in range(mrow // TILE):
            for across in range(ncol // TILE):
                keep = tiles_ref[down, across] != 0
                here = slice(down * TILE, (down + 1) * TILE), slice(across * TILE, (across + 1) * TILE)
                block = source[:, 0, here[0], here[1]]
                target[:, 0, here[0], here[1]] = jnp.where(keep, block, jnp.zeros_like(block))

    shape = (rows, 1, mrow, ncol)
    return pl.pallas_call(
        body,
        grid_spec=pltpu.PrefetchScalarGridSpec(
            num_scalar_prefetch=1,
            grid=(per,),
            in_specs=[pl.BlockSpec(shape, lambda i, t: (0, first + i, 0, 0))] + [ANY] * len(after),
            out_specs=pl.BlockSpec(shape, lambda i, t: (0, i, 0, 0)),
        ),
        out_shape=jax.ShapeDtypeStruct((rows, per, mrow, ncol), BF16),
        cost_estimate=cost(0, 4 * rows * per * mrow * ncol),
        compiler_params=params(),
        name="masked_piece",
    )(tiles, by_source, *after)


def masked_strips(coulomb, tiles, order, jpart, after):
    count = order.shape[0]
    pdev, mrow, ncol = coulomb.shape
    some = pdev // 4

    def body(order_ref, tiles_ref, *refs):
        ins, outs = refs[:count], refs[count + len(after) :]
        for step, (source, target) in enumerate(zip(ins, outs)):
            down = lax.div(order_ref[step] * jpart, TILE)
            for across in range(ncol // TILE):
                keep = tiles_ref[down, across] != 0
                span = slice(across * TILE, (across + 1) * TILE)
                block = source[:, :, span]
                target[:, :, span] = jnp.where(keep, block, jnp.zeros_like(block))

    def strip(step):
        return pl.BlockSpec((some, jpart, ncol), lambda p, order, tiles: (p, order[step], 0))

    return pl.pallas_call(
        body,
        grid_spec=pltpu.PrefetchScalarGridSpec(
            num_scalar_prefetch=2,
            grid=(pdev // some,),
            in_specs=[strip(step) for step in range(count)] + [ANY] * len(after),
            out_specs=[pl.BlockSpec((some, jpart, ncol), lambda p, order, tiles: (p, 0, 0))] * count,
        ),
        out_shape=[jax.ShapeDtypeStruct((pdev, jpart, ncol), BF16)] * count,
        cost_estimate=cost(0, 4 * count * pdev * jpart * ncol),
        compiler_params=params(),
        name="masked_strips",
    )(order, tiles, *([coulomb] * count), *after)


def occupied_order(whole, order, jpart, after):
    share, rows, _, part, nao = whole.shape
    mrow = share * part
    cols = order.shape[0]

    def body(order_ref, source, *refs):
        target, flipped = refs[len(after)], refs[len(after) + 1]
        flipped[...] = source[...].reshape(mrow, mrow).T
        for step in range(cols):
            first = pl.multiple_of(order_ref[step] * jpart, jpart)
            target[step, 0] = flipped[pl.ds(first, jpart), :]

    result = pl.pallas_call(
        body,
        grid_spec=pltpu.PrefetchScalarGridSpec(
            num_scalar_prefetch=1,
            grid=(rows, rows),
            in_specs=[pl.BlockSpec((share, 1, 1, part, mrow), lambda i, k, o: (0, k, 0, 0, i))]
            + [ANY] * len(after),
            out_specs=pl.BlockSpec((cols, 1, jpart, mrow), lambda i, k, o: (0, i, 0, k)),
            scratch_shapes=[pltpu.VMEM((mrow, mrow), BF16)],
        ),
        out_shape=jax.ShapeDtypeStruct((cols, rows, jpart, nao), BF16),
        cost_estimate=cost(0, 4 * nao * nao),
        compiler_params=params(),
        name="occupied_order",
    )(order, whole, *after)
    return result.reshape(nao, nao)


def virtual_order(whole, order, ncol, after):
    share, rows, _, part, nao = whole.shape
    cols = order.shape[0]
    units = ncol // part
    groups = share // units

    def body(order_ref, source, *refs):
        refs[len(after)][...] = source[...].reshape(ncol, ncol)

    return pl.pallas_call(
        body,
        grid_spec=pltpu.PrefetchScalarGridSpec(
            num_scalar_prefetch=1,
            grid=(cols, cols),
            in_specs=[
                pl.BlockSpec(
                    (units, 1, 1, part, ncol),
                    lambda i, k, o: (lax.rem(o[i], groups), lax.div(o[i], groups), 1, 0, o[k]),
                )
            ]
            + [ANY] * len(after),
            out_specs=pl.BlockSpec((ncol, ncol), lambda i, k, o: (i, k)),
        ),
        out_shape=jax.ShapeDtypeStruct((nao, nao), BF16),
        cost_estimate=cost(0, 4 * nao * nao),
        compiler_params=params(),
        name="virtual_order",
    )(order, whole, *after)


def contracted(returned, strips, first, after):
    rows, per, jpart, nao = returned.shape
    pdev, _, ncol = strips[0][0].shape
    left = rows * per
    group = min(jpart, 32 if left <= 8 else 16)
    tall = min(jpart, 32)
    steps = len(strips[0])
    count = len(strips) * steps
    flat = [value for half in strips for value in half]
    width, place = (ncol, first) if steps == 1 else (nao, 0)
    begin = first * ncol - place * width

    def body(returned_ref, *refs):
        ins, target = refs[:count], refs[count + len(after)]

        @pl.when(pl.program_id(0) == 0)
        def _():
            target[...] = jnp.zeros_like(target)

        shape = (group, left * group)
        equal = lax.broadcasted_iota(jnp.int32, shape, 0) == (
            lax.rem(lax.broadcasted_iota(jnp.int32, shape, 1), group)
        )
        for lower in range(0, tall, group):
            here = slice(lower, lower + group)
            mine = returned_ref[:, :, here, begin : begin + steps * ncol]
            mine = mine.reshape(left * group, steps * ncol)
            for half in range(len(strips)):
                other = [
                    ref[:, here, :].reshape(pdev * group, ncol)
                    for ref in ins[half * steps : (half + 1) * steps]
                ]
                total = lax.dot_general(
                    jnp.concatenate(other, axis=1),
                    mine,
                    (((1,), (1,)), ((), ())),
                    preferred_element_type=F32,
                )
                total = jnp.where(equal[None], total.reshape(pdev, group, left * group), 0.0)
                target[half] += jnp.sum(total, axis=1)

    result = pl.pallas_call(
        body,
        grid=(jpart // tall,),
        in_specs=[pl.BlockSpec((rows, per, tall, width), lambda i: (0, 0, i, place))]
        + [pl.BlockSpec((pdev, tall, ncol), lambda i: (0, i, 0))] * count
        + [ANY] * len(after),
        out_specs=pl.BlockSpec((len(strips), pdev, left * group), lambda i: (0, 0, 0)),
        out_shape=jax.ShapeDtypeStruct((len(strips), pdev, left * group), F32),
        cost_estimate=cost(
            2 * count * pdev * left * group * jpart * ncol,
            2 * jpart * ncol * (count * pdev + steps * left),
        ),
        compiler_params=params(),
        name="contracted",
    )(returned, *flat, *after)
    result = result.reshape(len(strips), pdev, rows, per, group).sum(axis=-1)
    return result.transpose(2, 3, 0, 1)


def half_transformed(occ_t, moved, first, per, parts, after):
    nao = occ_t.shape[0]
    rows, _, mrow, ncol = moved.shape
    span = nao // parts
    chunk = min(span, 256)

    def body(occ_ref, moved_ref, *refs):
        for part, target in enumerate(refs[len(after) :]):

            @pl.loop(0, span // chunk)
            def _(turn):
                local = pl.multiple_of(turn * chunk, chunk)
                here = pl.ds(pl.multiple_of(part * span + local, chunk), chunk)
                for one in range(per):
                    total = jnp.zeros((chunk, ncol), F32)
                    for row in range(rows):
                        left = occ_ref[here, row * mrow : (row + 1) * mrow]
                        total += jnp.dot(left, moved_ref[row, one], preferred_element_type=F32)
                    target[one, pl.ds(local, chunk), :] = total.astype(BF16)

    return pl.pallas_call(
        body,
        grid=(1,),
        in_specs=[
            pl.BlockSpec((nao, nao), lambda i: (0, 0), pipeline_mode=pl.Buffered(1)),
            pl.BlockSpec(
                (rows, per, mrow, ncol),
                lambda i: (0, first // per, 0, 0),
                pipeline_mode=pl.Buffered(1),
            ),
        ]
        + [ANY] * len(after),
        out_specs=[
            pl.BlockSpec((per, span, ncol), lambda i: (0, 0, 0), pipeline_mode=pl.Buffered(1))
        ]
        * parts,
        out_shape=[jax.ShapeDtypeStruct((per, span, ncol), BF16)] * parts,
        cost_estimate=cost(2 * per * nao * nao * ncol, 2 * nao * nao + 4 * per * nao * ncol),
        compiler_params=params(),
        name="half_transformed",
    )(occ_t, moved, *after)


def fully_transformed(blocks, virt, rows, base, index, total, after):
    nao = virt.shape[0]
    per, height, ncol = blocks[0].shape
    span = height // rows
    chunk = 256
    count = len(blocks)
    rest = ([] if base is None else [base]) + after

    def body(virt_ref, *refs):
        ins, target = refs[:count], refs[count + len(rest)]

        @pl.loop(0, nao // chunk)
        def _(turn):
            across = pl.ds(pl.multiple_of(turn * chunk, chunk), chunk)
            for one in range(per):
                total = jnp.zeros((height, chunk), F32)
                for step, block in enumerate(ins):
                    right = virt_ref[step * ncol : (step + 1) * ncol, across]
                    total += jnp.dot(block[one], right, preferred_element_type=F32)
                done = total.astype(BF16)
                for row in range(rows):
                    target[row, one, :, across] = done[row * span : (row + 1) * span]

    def alone(shape, place):
        return pl.BlockSpec(shape, lambda i: place, pipeline_mode=pl.Buffered(1))

    return pl.pallas_call(
        body,
        grid=(1,),
        in_specs=[alone((nao, nao), (0, 0))]
        + [alone((per, height, ncol), (0, 0, 0))] * count
        + [ANY] * len(rest),
        out_specs=alone((rows, per, span, nao), (0, index, 0, 0)),
        out_shape=jax.ShapeDtypeStruct((rows, total, span, nao), BF16),
        input_output_aliases={} if base is None else {1 + count: 0},
        cost_estimate=cost(2 * per * nao * nao * height, 2 * nao * nao + 4 * per * nao * height),
        compiler_params=params(),
        name="fully_transformed",
    )(virt, *blocks, *rest)


def shards(coulomb, occupied, virtual, tile_mask):
    rows = lax.axis_size("row")
    cols = lax.axis_size("col")
    pdev, mrow, ncol = coulomb.shape
    jpart = mrow // cols
    nao = mrow * rows
    mine = pdev // rows
    row_idx = lax.axis_index("row")
    col_idx = lax.axis_index("col")
    aux_idx = lax.axis_index("aux")
    col_order = col_idx ^ jnp.arange(cols, dtype=jnp.int32)
    tiles_r = mrow // TILE
    tiles_c = ncol // TILE
    tiles = lax.dynamic_slice(
        tile_mask, (row_idx * tiles_r, col_idx * tiles_c), (tiles_r, tiles_c)
    )
    by_source = coulomb.reshape(rows, mine, mrow, ncol)

    def along_row(value):
        return lax.all_to_all(value, "row", split_axis=0, concat_axis=0, tiled=True)

    def along_col(blocks):
        return [swapped(block, "col", step) for step, block in enumerate(blocks)]

    large, small = mine // 2, max(1, mine // 8)
    halves, last = large // 2, mine - large - small

    masked_small = masked_piece(by_source, tiles, large, small, [])
    masked_large = masked_piece(by_source, tiles, 0, large, [masked_small])
    masked_last = masked_piece(by_source, tiles, large + small, last, [masked_large])
    moved_small = along_row(masked_small)
    moved_large = along_row(masked_large)

    share = cols * lax.axis_size("aux")
    place = (col_idx * lax.axis_size("aux") + aux_idx).astype(jnp.int32)
    whole = own_parts([occupied, virtual], place, mrow // share, [moved_small, masked_large])
    whole = lax.all_gather(whole, "row", axis=0, tiled=False)
    whole = lax.all_gather(whole, ("col", "aux"), axis=0, tiled=False)
    occ_t = occupied_order(whole, col_order, jpart, [masked_last])
    virt = virtual_order(whole, col_order, ncol, [occ_t])

    half = half_transformed(occ_t, moved_small, 0, small, cols, [virt])
    first = fully_transformed(
        along_col(half), virt, rows, None, large // small, large + small, [half[0]]
    )
    released = ordered(masked_last, [moved_large, virt])
    moved_last = along_row(released)

    latest, spread = [released], []
    for number in range(2):
        half = half_transformed(occ_t, moved_large, number * halves, halves, cols, latest)
        latest = [half[0]]
        spread.append(along_col(half))
    for number, blocks in enumerate(spread):
        first = fully_transformed(
            blocks, virt, rows, first, number, large + small, latest if number == 0 else []
        )
    back = [along_row(first)]

    strips = masked_strips(coulomb, tiles, col_order[:-1], jpart, [first])
    strips = along_col(strips)
    theirs = [swapped(value, "aux", 1) for value in strips]

    half = half_transformed(occ_t, moved_last, 0, last, cols, [first])
    second = fully_transformed(
        along_col(half), virt, rows, None, 0, last, [half[0]] + strips[1:]
    )
    back.append(along_row(second))
    strips.append(swapped(masked_strips(coulomb, tiles, col_order[-1:], jpart, [second])[0], "col", cols - 1))
    theirs.append(swapped(strips[-1], "aux", 1))

    parts = [
        contracted(back[0], [strips[:-1], theirs[:-1]], 0, [second])
        + contracted(back[0], [strips[-1:], theirs[-1:]], cols - 1, [second]),
        contracted(back[1], [strips, theirs], 0, [second]),
    ]
    chi = jnp.concatenate(parts, axis=1)
    chi = jnp.where(aux_idx == 0, chi, chi[:, :, ::-1]).reshape(pdev, 2 * pdev)
    for axis, size in (("row", rows), ("col", cols)):
        chi = sum([swapped(chi, axis, step) for step in range(size)])
    return chi / NAO


def solution(mesh):
    placed = (P("aux", "row", "col"), P("row", None), P("row", None), P())
    return jax.shard_map(
        shards, mesh=mesh, in_specs=placed, out_specs=P("aux", None), check_vma=False
    )
```

profile of v0, /device:TPU:0, one launch (start us, length us, event | category | flops | bytes accessed | tf_op | source)
XLA Modules:
  0.0 877.6 jit_solution(10113454667824019827)
XLA Ops:
  11.3 6.3 all-to-all-start
  19.2 8.2 masked_piece.4.refs_3_.refs_0_
  27.4 38.4 %all-to-all-done.refs_2_.moved_ref = bf16[4,1,512,512]{3,2,1,0:T(8,128)(2,1)S(1)} async-done(((bf16[4,1,512,512]{3,2,1,0:T(8,128)(2,1)}), bf16[4,1,512,512]{3,2,1,0:T(8,128)(2,1)S(1)}, u32[]{:S(2)}, u32[]{:S(2)}) %all-to-all-start) | async-done | bytes 2097184 | tf_op jit(solution)/shard_map/all_to_all | solution.py:351
  69.1 45.2 %all-gather.5.cloned.1.call-done = bf16[8,64,2048]{2,1,0:T(8,128)(2,1)} async-done(((bf16[2,64,2048]{2,1,0:T(8,128)(2,1)}), bf16[8,64,2048]{2,1,0:T(8,128)(2,1)}) %all-gather.5.cloned.1.call-update) | async-done | bytes 2097168 | tf_op jit(solution)/shard_map/all_gather | solution.py:368
  114.3 5.7 all-to-all-start.1
  120.0 8.2 masked_piece.5.refs_0_
  128.2 76.6 %all-gather.7.cloned.1.call-done = bf16[32,2,64,2048]{3,2,1,0:T(8,128)(2,1)} async-done(((bf16[4,2,64,2048]{3,2,1,0:T(8,128)(2,1)}), bf16[32,2,64,2048]{3,2,1,0:T(8,128)(2,1)}) %all-gather.7.cloned.1.call-update) | async-done | bytes 16777232 | tf_op jit(solution)/shard_map/all_gather | solution.py:369
  204.7 14.1 %occupied_order.1 = bf16[4,4,128,2048]{3,2,1,0:T(8,128)(2,1)} custom-call(s32[4]{0:T(128)S(1)} %iota_xor_fusion.order_ref, bf16[8,4,2,64,2048]{4,3,2,1,0:T(8,128)(2,1)} %bitcast.21, bf16[4,3,512,512]{3,2,1,0:T(8,128)(2,1)} %masked_piece.5.refs_0_), custom_call_target="tpu_custom_call" | custom-call | bytes 16777216 | tf_op jit(solution)/shard_map/occupied_order/pallas_call | solution.py:140
  218.8 12.6 %virtual_order.1.refs_2_.refs_0_.virt_ref = bf16[2048,2048]{1,0:T(8,128)(2,1)} custom-call(s32[4]{0:T(128)S(1)} %iota_xor_fusion.order_ref, bf16[8,4,2,64,2048]{4,3,2,1,0:T(8,128)(2,1)} %bitcast.22, bf16[2048,2048]{1,0:T(8,128)(2,1)} %bitcast.16), custom_call_target="tpu_custom_call" | custom-call | bytes 16777216 | tf_op jit(solution)/shard_map/virtual_order/pallas_call | solution.py:167
  231.5 71.8 %all-to-all-done.1.refs_1_.moved_ref = bf16[4,4,512,512]{3,2,1,0:T(8,128)(2,1)} async-done(((bf16[4,4,512,512]{3,2,1,0:T(8,128)(2,1)}), bf16[4,4,512,512]{3,2,1,0:T(8,128)(2,1)}, u32[]{:S(2)}, u32[]{:S(2)}) %all-to-all-start.1) | async-done | bytes 8388640 | tf_op jit(solution)/shard_map/all_to_all | solution.py:351
  308.9 9.2 %half_transformed.6 = (bf16[1,512,512]{2,1,0:T(8,128)(2,1)S(1)}, bf16[1,512,512]{2,1,0:T(8,128)(2,1)S(1)}, bf16[1,512,512]{2,1,0:T(8,128)(2,1)S(1)}, bf16[1,512,512]{2,1,0:T(8,128)(2,1)S(1)}) custom-call(bf16[2048,2048]{1,0:T(8,128)(2,1)} %bitcast.17, bf16[4,1,512,512]{3,2,1,0:T(8,128)(2,1)S(1)} %copy-done.1, ...), custom_call_target="tpu_custom_call" | custom-call | flops 4294967296 | bytes 12582912 | tf_op jit(solution)/shard_map/half_transformed/pallas_call | solution.py:268
  319.6 14.8 %half_transformed.4 = (bf16[2,512,512]{2,1,0:T(8,128)(2,1)S(1)}, bf16[2,512,512]{2,1,0:T(8,128)(2,1)S(1)}, bf16[2,512,512]{2,1,0:T(8,128)(2,1)S(1)}, bf16[2,512,512]{2,1,0:T(8,128)(2,1)S(1)}) custom-call(bf16[2048,2048]{1,0:T(8,128)(2,1)} %bitcast.18, bf16[4,4,512,512]{3,2,1,0:T(8,128)(2,1)} %all-to-all-done.1.refs_1_.moved_ref, ...), custom_call_target="tpu_custom_call" | custom-call | flops 8589934592 | bytes 16777216 | tf_op jit(solution)/shard_map/half_transformed/pallas_call | solution.py:268
  340.0 14.8 %half_transformed.5 = (bf16[2,512,512]{2,1,0:T(8,128)(2,1)S(1)}, bf16[2,512,512]{2,1,0:T(8,128)(2,1)}, bf16[2,512,512]{2,1,0:T(8,128)(2,1)S(1)}, bf16[2,512,512]{2,1,0:T(8,128)(2,1)S(1)}) custom-call(bf16[2048,2048]{1,0:T(8,128)(2,1)} %bitcast.19, bf16[4,4,512,512]{3,2,1,0:T(8,128)(2,1)} %all-to-all-done.1.refs_1_.moved_ref, ...), custom_call_target="tpu_custom_call" | custom-call | flops 8589934592 | bytes 16777216 | tf_op jit(solution)/shard_map/half_transformed/pallas_call | solution.py:268
  356.4 16.4 %collective-permute-done.8.refs_3_ = bf16[1,512,512]{2,1,0:T(8,128)(2,1)S(1)} collective-permute-done((bf16[1,512,512]{2,1,0:T(8,128)(2,1)S(1)}, bf16[1,512,512]{2,1,0:T(8,128)(2,1)S(1)}, u32[]{:S(2)}, u32[]{:S(2)}) %collective-permute-start.8) | collective-permute-done | bytes 524320 | tf_op jit(solution)/shard_map/ppermute | solution.py:21
  374.8 10.6 %fully_transformed.4.refs_4_ = bf16[4,5,128,2048]{3,2,1,0:T(8,128)(2,1)} custom-call(bf16[2048,2048]{1,0:T(8,128)(2,1)} %virtual_order.1.refs_2_.refs_0_.virt_ref, bf16[1,512,512]{2,1,0:T(8,128)(2,1)S(1)} %get-tuple-element.32.refs_0_.refs_4_, bf16[1,512,512]{2,1,0:T(8,128)(2,1)S(1)} %collective-permute-done.6.refs_1_, ...), custom_call_target="tpu_custom_call" | custom-call | flops 4294967296 | bytes 12582912 | tf_op jit(solution)/shard_map/fully_transformed/pallas_call | solution.py:317
  385.5 20.6 %collective-permute-done.4.refs_2_ = bf16[2,512,512]{2,1,0:T(8,128)(2,1)S(1)} collective-permute-done((bf16[2,512,512]{2,1,0:T(8,128)(2,1)S(1)}, bf16[2,512,512]{2,1,0:T(8,128)(2,1)S(1)}, u32[]{:S(2)}, u32[]{:S(2)}) %collective-permute-start.4) | collective-permute-done | bytes 1048608 | tf_op jit(solution)/shard_map/ppermute | solution.py:21
  406.1 15.4 %fully_transformed.5.refs_4_ = bf16[4,5,128,2048]{3,2,1,0:T(8,128)(2,1)} custom-call(bf16[2048,2048]{1,0:T(8,128)(2,1)} %virtual_order.1.refs_2_.refs_0_.virt_ref, bf16[2,512,512]{2,1,0:T(8,128)(2,1)S(1)} %get-tuple-element.24.refs_0_, bf16[2,512,512]{2,1,0:T(8,128)(2,1)S(1)} %collective-permute-done.3.refs_1_, ...), custom_call_target="tpu_custom_call", output_to_operand_aliasing={{}: (5, {})} | custom-call | flops 8589934592 | bytes 16777216 | tf_op jit(solution)/shard_map/fully_transformed/pallas_call | solution.py:317
  421.5 27.1 %collective-permute-done.1.refs_2_ = bf16[2,512,512]{2,1,0:T(8,128)(2,1)S(1)} collective-permute-done((bf16[2,512,512]{2,1,0:T(8,128)(2,1)S(1)}, bf16[2,512,512]{2,1,0:T(8,128)(2,1)S(1)}, u32[]{:S(2)}, u32[]{:S(2)}) %collective-permute-start.1) | collective-permute-done | bytes 1048608 | tf_op jit(solution)/shard_map/ppermute | solution.py:21
  448.6 15.4 %fully_transformed.6.refs_3_.refs_0_ = bf16[4,5,128,2048]{3,2,1,0:T(8,128)(2,1)} custom-call(bf16[2048,2048]{1,0:T(8,128)(2,1)} %virtual_order.1.refs_2_.refs_0_.virt_ref, bf16[2,512,512]{2,1,0:T(8,128)(2,1)S(1)} %get-tuple-element.25.refs_5_.refs_0_, bf16[2,512,512]{2,1,0:T(8,128)(2,1)S(1)} %collective-permute-done.refs_1_, ...), custom_call_target="tpu_custom_call", output_to_operand_aliasing={{}: (5, {})} | custom-call | flops 8589934592 | bytes 16777216 | tf_op jit(solution)/shard_map/fully_transformed/pallas_call | solution.py:317
  463.9 6.2 all-to-all-start.2
  470.1 10.7 %masked_strips.2 = (bf16[32,128,512]{2,1,0:T(8,128)(2,1)}, bf16[32,128,512]{2,1,0:T(8,128)(2,1)}, bf16[32,128,512]{2,1,0:T(8,128)(2,1)}) custom-call(s32[3]{0:T(128)S(1)} %bitcast.12, s32[4,4]{1,0:T(4,128)S(1)} %dynamic_slice.3.tiles_ref, bf16[32,512,512]{2,1,0:T(8,128)(2,1)} %refs_0_.5, bf16[32,512,512]{2,1,0:T(8,128)(2,1)} %refs_0_.5, ...), custom_call_target="tpu_custom_call" | custom-call | bytes 25165824 | tf_op jit(solution)/shard_map/masked_strips/pallas_call | solution.py:113
  483.7 21.1 %half_transformed.7 = (bf16[3,512,512]{2,1,0:T(8,128)(2,1)S(1)}, bf16[3,512,512]{2,1,0:T(8,128)(2,1)S(1)}, bf16[3,512,512]{2,1,0:T(8,128)(2,1)S(1)}, bf16[3,512,512]{2,1,0:T(8,128)(2,1)}) custom-call(bf16[2048,2048]{1,0:T(8,128)(2,1)} %bitcast.20, bf16[4,3,512,512]{3,2,1,0:T(8,128)(2,1)} %all-to-all-done.3.moved_ref, ...), custom_call_target="tpu_custom_call" | custom-call | flops 12884901888 | bytes 20971520 | tf_op jit(solution)/shard_map/half_transformed/pallas_call | solution.py:268
  508.3 66.4 %collective-permute-done.10.refs_6_.refs_2_ = bf16[32,128,512]{2,1,0:T(8,128)(2,1)} collective-permute-done((bf16[32,128,512]{2,1,0:T(8,128)(2,1)}, bf16[32,128,512]{2,1,0:T(8,128)(2,1)}, u32[]{:S(2)}, u32[]{:S(2)}) %collective-permute-start.10) | collective-permute-done | bytes 4194336 | tf_op jit(solution)/shard_map/ppermute | solution.py:21
  576.1 33.6 %collective-permute-done.14.refs_1_ = bf16[3,512,512]{2,1,0:T(8,128)(2,1)S(1)} collective-permute-done((bf16[3,512,512]{2,1,0:T(8,128)(2,1)S(1)}, bf16[3,512,512]{2,1,0:T(8,128)(2,1)S(1)}, u32[]{:S(2)}, u32[]{:S(2)}) %collective-permute-start.14) | collective-permute-done | bytes 1572896 | tf_op jit(solution)/shard_map/ppermute | solution.py:21
  609.7 30.1 %collective-permute-done.16.refs_3_ = bf16[3,512,512]{2,1,0:T(8,128)(2,1)S(1)} collective-permute-done((bf16[3,512,512]{2,1,0:T(8,128)(2,1)}, bf16[3,512,512]{2,1,0:T(8,128)(2,1)S(1)}, u32[]{:S(2)}, u32[]{:S(2)}) %collective-permute-start.16) | collective-permute-done | bytes 1572896 | tf_op jit(solution)/shard_map/ppermute | solution.py:21
  641.0 21.1 %fully_transformed.7.refs_6_.refs_1_.refs_2_.refs_8_ = bf16[4,3,128,2048]{3,2,1,0:T(8,128)(2,1)} custom-call(bf16[2048,2048]{1,0:T(8,128)(2,1)} %virtual_order.1.refs_2_.refs_0_.virt_ref, bf16[3,512,512]{2,1,0:T(8,128)(2,1)S(1)} %get-tuple-element.39.refs_0_.refs_4_, bf16[3,512,512]{2,1,0:T(8,128)(2,1)S(1)} %collective-permute-done.14.refs_1_, ...), custom_call_target="tpu_custom_call" | custom-call | flops 12884901888 | bytes 20971520 | tf_op jit(solution)/shard_map/fully_transformed/pallas_call | solution.py:317
  662.1 34.0 %all-to-all-done.2.returned_ref = bf16[4,5,128,2048]{3,2,1,0:T(8,128)(2,1)} async-done(((bf16[4,5,128,2048]{3,2,1,0:T(8,128)(2,1)}), bf16[4,5,128,2048]{3,2,1,0:T(8,128)(2,1)}, u32[]{:S(2)}, u32[]{:S(2)}) %all-to-all-start.2) | async-done | bytes 10485792 | tf_op jit(solution)/shard_map/all_to_all | solution.py:351
  709.6 89.7 %collective-permute-done.17.refs_0_.refs_3_ = bf16[32,128,512]{2,1,0:T(8,128)(2,1)} collective-permute-done((bf16[32,128,512]{2,1,0:T(8,128)(2,1)S(1)}, bf16[32,128,512]{2,1,0:T(8,128)(2,1)}, u32[]{:S(2)}, u32[]{:S(2)}) %collective-permute-start.17) | collective-permute-done | bytes 4194336 | tf_op jit(solution)/shard_map/ppermute | solution.py:21
  799.4 17.5 %contracted.3 = f32[2,32,320]{2,1,0:T(8,128)S(1)} custom-call(bf16[4,5,128,2048]{3,2,1,0:T(8,128)(2,1)} %all-to-all-done.2.returned_ref, bf16[32,128,512]{2,1,0:T(8,128)(2,1)} %get-tuple-element.36.refs_0_, bf16[32,128,512]{2,1,0:T(8,128)(2,1)} %collective-permute-done.9.refs_5_.refs_1_, bf16[32,128,512]{2,1,0:T(8,128)(2,1)} %collective-permute-done.10.refs_6_.refs_2_, ...), custom_call_target="tpu_custom_call" | custom-call | flops 8053063680 | bytes 33030144 | tf_op jit(solution)/shard_map/contracted/pallas_call | solution.py:229
  817.1 7.5 contracted.4
  824.9 14.2 %all-to-all-done.4.returned_ref = bf16[4,3,128,2048]{3,2,1,0:T(8,128)(2,1)} async-done(((bf16[4,3,128,2048]{3,2,1,0:T(8,128)(2,1)}), bf16[4,3,128,2048]{3,2,1,0:T(8,128)(2,1)}, u32[]{:S(2)}, u32[]{:S(2)}) %all-to-all-start.4) | async-done | bytes 6291488 | tf_op jit(solution)/shard_map/all_to_all | solution.py:351
  839.0 15.7 %contracted.5 = f32[2,32,192]{2,1,0:T(8,128)S(1)} custom-call(bf16[4,3,128,2048]{3,2,1,0:T(8,128)(2,1)} %all-to-all-done.4.returned_ref, bf16[32,128,512]{2,1,0:T(8,128)(2,1)} %get-tuple-element.36.refs_0_, bf16[32,128,512]{2,1,0:T(8,128)(2,1)} %collective-permute-done.9.refs_5_.refs_1_, bf16[32,128,512]{2,1,0:T(8,128)(2,1)} %collective-permute-done.10.refs_6_.refs_2_, ...), custom_call_target="tpu_custom_call" | custom-call | flops 6442450944 | bytes 39845888 | tf_op jit(solution)/shard_map/contracted/pallas_call | solution.py:229
  (80 shorter events, 64.8 us)
Async XLA Ops:
  11.3 54.5 %all-to-all-start = ((bf16[4,1,512,512]{3,2,1,0:T(8,128)(2,1)}), bf16[4,1,512,512]{3,2,1,0:T(8,128)(2,1)S(1)}, u32[]{:S(2)}, u32[]{:S(2)}) async-start(bf16[4,1,512,512]{3,2,1,0:T(8,128)(2,1)} %copy-done.2), calls=%async_computation | async-start | bytes 4194304 | tf_op jit(solution)/shard_map/all_to_all | solution.py:351
  17.6 96.6 %all-gather.5.cloned.1.call-start = ((), (), s32[]{:S(2)}) async-start(), calls=%async_computation.5 | async-start | bytes 2621440 | tf_op jit(solution)/shard_map/all_gather | solution.py:368
  69.0 135.7 %all-gather.7.cloned.1.call-start = ((), (), s32[]{:S(2)}) async-start(), calls=%async_computation.6 | async-start | bytes 18874368 | tf_op jit(solution)/shard_map/all_gather | solution.py:369
  114.3 189.1 %all-to-all-start.1 = ((bf16[4,4,512,512]{3,2,1,0:T(8,128)(2,1)}), bf16[4,4,512,512]{3,2,1,0:T(8,128)(2,1)}, u32[]{:S(2)}, u32[]{:S(2)}) async-start(bf16[4,4,512,512]{3,2,1,0:T(8,128)(2,1)} %masked_piece.4.refs_3_.refs_0_), calls=%async_computation.1 | async-start | bytes 16777216 | tf_op jit(solution)/shard_map/all_to_all | solution.py:351
  303.3 160.6 %all-to-all-start.3 = ((bf16[4,3,512,512]{3,2,1,0:T(8,128)(2,1)}), bf16[4,3,512,512]{3,2,1,0:T(8,128)(2,1)}, u32[]{:S(2)}, u32[]{:S(2)}) async-start(bf16[4,3,512,512]{3,2,1,0:T(8,128)(2,1)} %ordered.1.refs_0_), calls=%async_computation.3 | async-start | bytes 12582912 | tf_op jit(solution)/shard_map/all_to_all | solution.py:351
  318.1 21.4 %collective-permute-start.6 = (bf16[1,512,512]{2,1,0:T(8,128)(2,1)S(1)}, bf16[1,512,512]{2,1,0:T(8,128)(2,1)S(1)}, u32[]{:S(2)}, u32[]{:S(2)}) collective-permute-start(bf16[1,512,512]{2,1,0:T(8,128)(2,1)S(1)} %get-tuple-element.33), channel_id=1, source_target_pairs={{0,1},{1,0},{2,3},{3,2},{4,5},{5,4},{6,7},{7,6},{8,9},{9,8},{10,11... | collective-permute-start | bytes 1572872 | tf_op jit(solution)/shard_map/ppermute | solution.py:21
  334.4 39.0 %collective-permute-start.3 = (bf16[2,512,512]{2,1,0:T(8,128)(2,1)S(1)}, bf16[2,512,512]{2,1,0:T(8,128)(2,1)S(1)}, u32[]{:S(2)}, u32[]{:S(2)}) collective-permute-start(bf16[2,512,512]{2,1,0:T(8,128)(2,1)S(1)} %get-tuple-element.29), channel_id=1, source_target_pairs={{0,1},{1,0},{2,3},{3,2},{4,5},{5,4},{6,7},{7,6},{8,9},{9,8},{10,11... | collective-permute-start | bytes 3145736 | tf_op jit(solution)/shard_map/ppermute | solution.py:21
  335.1 19.8 %collective-permute-start.7 = (bf16[1,512,512]{2,1,0:T(8,128)(2,1)S(1)}, bf16[1,512,512]{2,1,0:T(8,128)(2,1)S(1)}, u32[]{:S(2)}, u32[]{:S(2)}) collective-permute-start(bf16[1,512,512]{2,1,0:T(8,128)(2,1)S(1)} %get-tuple-element.34), channel_id=1, source_target_pairs={{0,2},{1,3},{2,0},{3,1},{4,6},{5,7},{6,4},{7,5},{8,10},{9,11},{10,... | collective-permute-start | bytes 1572872 | tf_op jit(solution)/shard_map/ppermute | solution.py:21
  336.5 36.3 %collective-permute-start.8 = (bf16[1,512,512]{2,1,0:T(8,128)(2,1)S(1)}, bf16[1,512,512]{2,1,0:T(8,128)(2,1)S(1)}, u32[]{:S(2)}, u32[]{:S(2)}) collective-permute-start(bf16[1,512,512]{2,1,0:T(8,128)(2,1)S(1)} %get-tuple-element.35), channel_id=1, source_target_pairs={{0,3},{1,2},{2,1},{3,0},{4,7},{5,6},{6,5},{7,4},{8,11},{9,10},{10,... | collective-permute-start | bytes 1572872 | tf_op jit(solution)/shard_map/ppermute | solution.py:21
  338.0 68.1 %collective-permute-start.4 = (bf16[2,512,512]{2,1,0:T(8,128)(2,1)S(1)}, bf16[2,512,512]{2,1,0:T(8,128)(2,1)S(1)}, u32[]{:S(2)}, u32[]{:S(2)}) collective-permute-start(bf16[2,512,512]{2,1,0:T(8,128)(2,1)S(1)} %get-tuple-element.30), channel_id=1, source_target_pairs={{0,2},{1,3},{2,0},{3,1},{4,6},{5,7},{6,4},{7,5},{8,10},{9,11},{10,... | collective-permute-start | bytes 3145736 | tf_op jit(solution)/shard_map/ppermute | solution.py:21
  339.4 66.7 %collective-permute-start.5 = (bf16[2,512,512]{2,1,0:T(8,128)(2,1)S(1)}, bf16[2,512,512]{2,1,0:T(8,128)(2,1)S(1)}, u32[]{:S(2)}, u32[]{:S(2)}) collective-permute-start(bf16[2,512,512]{2,1,0:T(8,128)(2,1)S(1)} %get-tuple-element.31), channel_id=1, source_target_pairs={{0,3},{1,2},{2,1},{3,0},{4,7},{5,6},{6,5},{7,4},{8,11},{9,10},{10,... | collective-permute-start | bytes 3145736 | tf_op jit(solution)/shard_map/ppermute | solution.py:21
  354.9 66.6 %collective-permute-start = (bf16[2,512,512]{2,1,0:T(8,128)(2,1)}, bf16[2,512,512]{2,1,0:T(8,128)(2,1)S(1)}, u32[]{:S(2)}, u32[]{:S(2)}) collective-permute-start(bf16[2,512,512]{2,1,0:T(8,128)(2,1)} %get-tuple-element.26), channel_id=1, source_target_pairs={{0,1},{1,0},{2,3},{3,2},{4,5},{5,4},{6,7},{7,6},{8,9},{9,8},{10,11... | collective-permute-start | bytes 3145736 | tf_op jit(solution)/shard_map/ppermute | solution.py:21
  372.8 75.7 %collective-permute-start.1 = (bf16[2,512,512]{2,1,0:T(8,128)(2,1)S(1)}, bf16[2,512,512]{2,1,0:T(8,128)(2,1)S(1)}, u32[]{:S(2)}, u32[]{:S(2)}) collective-permute-start(bf16[2,512,512]{2,1,0:T(8,128)(2,1)S(1)} %get-tuple-element.27), channel_id=1, source_target_pairs={{0,2},{1,3},{2,0},{3,1},{4,6},{5,7},{6,4},{7,5},{8,10},{9,11},{10,... | collective-permute-start | bytes 3145736 | tf_op jit(solution)/shard_map/ppermute | solution.py:21
  373.4 75.1 %collective-permute-start.2 = (bf16[2,512,512]{2,1,0:T(8,128)(2,1)S(1)}, bf16[2,512,512]{2,1,0:T(8,128)(2,1)S(1)}, u32[]{:S(2)}, u32[]{:S(2)}) collective-permute-start(bf16[2,512,512]{2,1,0:T(8,128)(2,1)S(1)} %get-tuple-element.28), channel_id=1, source_target_pairs={{0,3},{1,2},{2,1},{3,0},{4,7},{5,6},{6,5},{7,4},{8,11},{9,10},{10,... | collective-permute-start | bytes 3145736 | tf_op jit(solution)/shard_map/ppermute | solution.py:21
  463.9 232.2 %all-to-all-start.2 = ((bf16[4,5,128,2048]{3,2,1,0:T(8,128)(2,1)}), bf16[4,5,128,2048]{3,2,1,0:T(8,128)(2,1)}, u32[]{:S(2)}, u32[]{:S(2)}) async-start(bf16[4,5,128,2048]{3,2,1,0:T(8,128)(2,1)} %fully_transformed.6.refs_3_.refs_0_), calls=%async_computation.2 | async-start | bytes 20971520 | tf_op jit(solution)/shard_map/all_to_all | solution.py:351
  480.8 93.8 %collective-permute-start.10 = (bf16[32,128,512]{2,1,0:T(8,128)(2,1)}, bf16[32,128,512]{2,1,0:T(8,128)(2,1)}, u32[]{:S(2)}, u32[]{:S(2)}) collective-permute-start(bf16[32,128,512]{2,1,0:T(8,128)(2,1)} %get-tuple-element.38), channel_id=1, source_target_pairs={{0,2},{1,3},{2,0},{3,1},{4,6},{5,7},{6,4},{7,5},{8,10},{9,11},{10,... | collective-permute-start | bytes 12582920 | tf_op jit(solution)/shard_map/ppermute | solution.py:21
  482.3 93.8 %collective-permute-start.9 = (bf16[32,128,512]{2,1,0:T(8,128)(2,1)}, bf16[32,128,512]{2,1,0:T(8,128)(2,1)}, u32[]{:S(2)}, u32[]{:S(2)}) collective-permute-start(bf16[32,128,512]{2,1,0:T(8,128)(2,1)} %get-tuple-element.37), channel_id=1, source_target_pairs={{0,1},{1,0},{2,3},{3,2},{4,5},{5,4},{6,7},{7,6},{8,9},{9,8},{10,11... | collective-permute-start | bytes 12582920 | tf_op jit(solution)/shard_map/ppermute | solution.py:21
  504.8 104.9 %collective-permute-start.14 = (bf16[3,512,512]{2,1,0:T(8,128)(2,1)S(1)}, bf16[3,512,512]{2,1,0:T(8,128)(2,1)S(1)}, u32[]{:S(2)}, u32[]{:S(2)}) collective-permute-start(bf16[3,512,512]{2,1,0:T(8,128)(2,1)S(1)} %get-tuple-element.40), channel_id=1, source_target_pairs={{0,1},{1,0},{2,3},{3,2},{4,5},{5,4},{6,7},{7,6},{8,9},{9,8},{10,11... | collective-permute-start | bytes 4718600 | tf_op jit(solution)/shard_map/ppermute | solution.py:21
  505.4 104.3 %collective-permute-start.15 = (bf16[3,512,512]{2,1,0:T(8,128)(2,1)S(1)}, bf16[3,512,512]{2,1,0:T(8,128)(2,1)S(1)}, u32[]{:S(2)}, u32[]{:S(2)}) collective-permute-start(bf16[3,512,512]{2,1,0:T(8,128)(2,1)S(1)} %get-tuple-element.41), channel_id=1, source_target_pairs={{0,2},{1,3},{2,0},{3,1},{4,6},{5,7},{6,4},{7,5},{8,10},{9,11},{10,... | collective-permute-start | bytes 4718600 | tf_op jit(solution)/shard_map/ppermute | solution.py:21
  506.0 133.9 %collective-permute-start.16 = (bf16[3,512,512]{2,1,0:T(8,128)(2,1)}, bf16[3,512,512]{2,1,0:T(8,128)(2,1)S(1)}, u32[]{:S(2)}, u32[]{:S(2)}) collective-permute-start(bf16[3,512,512]{2,1,0:T(8,128)(2,1)} %get-tuple-element.42), channel_id=1, source_target_pairs={{0,3},{1,2},{2,1},{3,0},{4,7},{5,6},{6,5},{7,4},{8,11},{9,10},{10,... | collective-permute-start | bytes 4718600 | tf_op jit(solution)/shard_map/ppermute | solution.py:21
  696.1 142.9 %all-to-all-start.4 = ((bf16[4,3,128,2048]{3,2,1,0:T(8,128)(2,1)}), bf16[4,3,128,2048]{3,2,1,0:T(8,128)(2,1)}, u32[]{:S(2)}, u32[]{:S(2)}) async-start(bf16[4,3,128,2048]{3,2,1,0:T(8,128)(2,1)} %fully_transformed.7.refs_6_.refs_1_.refs_2_.refs_8_), calls=%async_computation.4 | async-start | bytes 12582912 | tf_op jit(solution)/shard_map/all_to_all | solution.py:351
  706.8 92.6 %collective-permute-start.17 = (bf16[32,128,512]{2,1,0:T(8,128)(2,1)S(1)}, bf16[32,128,512]{2,1,0:T(8,128)(2,1)}, u32[]{:S(2)}, u32[]{:S(2)}) collective-permute-start(bf16[32,128,512]{2,1,0:T(8,128)(2,1)S(1)} %masked_strips.3), channel_id=1, source_target_pairs={{0,3},{1,2},{2,1},{3,0},{4,7},{5,6},{6,5},{7,4},{8,11},{9,10},{10,... | collective-permute-start | bytes 12582920 | tf_op jit(solution)/shard_map/ppermute | solution.py:21
  709.1 90.3 %collective-permute-start.11 = (bf16[32,128,512]{2,1,0:T(8,128)(2,1)}, bf16[32,128,512]{2,1,0:T(8,128)(2,1)}, u32[]{:S(2)}, u32[]{:S(2)}) collective-permute-start(bf16[32,128,512]{2,1,0:T(8,128)(2,1)} %get-tuple-element.36.refs_0_), channel_id=1, source_target_pairs={{0,16},{16,0},{1,17},{17,1},{2,18},{18,2},{3,19},{19,3},{4,20},{20... | collective-permute-start | bytes 12582920 | tf_op jit(solution)/shard_map/ppermute | solution.py:21
  709.1 90.3 %collective-permute-start.12 = (bf16[32,128,512]{2,1,0:T(8,128)(2,1)}, bf16[32,128,512]{2,1,0:T(8,128)(2,1)}, u32[]{:S(2)}, u32[]{:S(2)}) collective-permute-start(bf16[32,128,512]{2,1,0:T(8,128)(2,1)} %collective-permute-done.9.refs_5_.refs_1_), channel_id=1, source_target_pairs={{0,16},{16,0},{1,17},{17,1},{2,18},{18,2},{3,19},{19,3},{4,20},{20... | collective-permute-start | bytes 12582920 | tf_op jit(solution)/shard_map/ppermute | solution.py:21
  709.6 89.8 %collective-permute-start.13 = (bf16[32,128,512]{2,1,0:T(8,128)(2,1)}, bf16[32,128,512]{2,1,0:T(8,128)(2,1)}, u32[]{:S(2)}, u32[]{:S(2)}) collective-permute-start(bf16[32,128,512]{2,1,0:T(8,128)(2,1)} %collective-permute-done.10.refs_6_.refs_2_), channel_id=1, source_target_pairs={{0,16},{16,0},{1,17},{17,1},{2,18},{18,2},{3,19},{19,3},{4,20},{20... | collective-permute-start | bytes 12582920 | tf_op jit(solution)/shard_map/ppermute | solution.py:21
  799.4 17.7 %collective-permute-start.18 = (bf16[32,128,512]{2,1,0:T(8,128)(2,1)}, bf16[32,128,512]{2,1,0:T(8,128)(2,1)}, u32[]{:S(2)}, u32[]{:S(2)}) collective-permute-start(bf16[32,128,512]{2,1,0:T(8,128)(2,1)} %collective-permute-done.17.refs_0_.refs_3_), channel_id=1, source_target_pairs={{0,16},{16,0},{1,17},{17,1},{2,18},{18,2},{3,19},{19,3},{4,20},{20... | collective-permute-start | bytes 12582920 | tf_op jit(solution)/shard_map/ppermute | solution.py:21
  855.1 4.4 collective-permute-start.19
  855.1 4.7 collective-permute-start.20
  857.1 5.5 collective-permute-start.21
  862.7 3.7 collective-permute-start.22
  864.1 3.7 collective-permute-start.23
  865.5 4.6 collective-permute-start.24
  (5 other events, 11.1 us)
Sparse Core Ops, SparseCore 0:
  69.2 45.0 all-gather.4
  116.1 88.5 all-gather.6
where the time goes:
time: 879 us; the launch traced here: 878 us
  waiting for transfers between devices  573 us (65%)
  Pallas kernels  226 us (26%)
  starting transfers between devices  57 us (6%)
  between operations  13.6 us (2%)
    ppermute x25, waiting for transfers between devices, swapped(): return lax.ppermute(value, axis, pairs)  293 us
    all_to_all x5, waiting for transfers between devices, along_row(): return lax.all_to_all(value, 'row', split_axis=0, concat_axis=0, tiled=True)  158 us
    all_gather x1, waiting for transfers between devices, shards(): whole = lax.all_gather(whole, ('col', 'aux'), axis=0, tiled=False)  76.6 us
    pallas_call x4, Pallas kernels, fully_transformed(): pl.pallas_call(body, grid=(1,), in_specs=[alone((nao, nao), (0, 0))] + [a...  62.5 us
    pallas_call x4, Pallas kernels, half_transformed(): pl.pallas_call(body, grid=(1,), in_specs=[pl.BlockSpec((nao, nao), lambda...  59.9 us
    all_gather x1, waiting for transfers between devices, shards(): whole = lax.all_gather(whole, 'row', axis=0, tiled=False)  45.2 us
    pallas_call x3, Pallas kernels, contracted(): pl.pallas_call(body, grid=(jpart // tall,), in_specs=[pl.BlockSpec((rows,...  40.7 us
    all_to_all x5, starting transfers between devices, along_row(): return lax.all_to_all(value, 'row', split_axis=0, concat_axis=0, tiled=True)  29.2 us
  transfers between devices with their start and end apart: 32, of which 19 were waited for; matrix products, arithmetic and copies ran while one was open for 0% of the time, Pallas kernels for 23%

commit v1 on v0

--- a/solution.py
+++ b/solution.py
@@ -364,8 +364,9 @@
 
     share = cols * lax.axis_size("aux")
     place = (col_idx * lax.axis_size("aux") + aux_idx).astype(jnp.int32)
-    whole = own_parts([occupied, virtual], place, mrow // share, [moved_small, masked_large])
+    whole = own_parts([occupied, virtual], place, mrow // share, [masked_small])
     whole = lax.all_gather(whole, "row", axis=0, tiled=False)
+    whole = ordered(whole, [moved_small, masked_large])
     whole = lax.all_gather(whole, ("col", "aux"), axis=0, tiled=False)
     occ_t = occupied_order(whole, col_order, jpart, [masked_last])
     virt = virtual_order(whole, col_order, ncol, [occ_t])
@@ -374,7 +375,7 @@
     first = fully_transformed(
         along_col(half), virt, rows, None, large // small, large + small, [half[0]]
     )
-    released = ordered(masked_last, [moved_large, virt])
+    released = ordered(masked_last, [moved_large, first])
     moved_last = along_row(released)
 
     latest, spread = [released], []
@@ -407,8 +408,9 @@
     ]
     chi = jnp.concatenate(parts, axis=1)
     chi = jnp.where(aux_idx == 0, chi, chi[:, :, ::-1]).reshape(pdev, 2 * pdev)
-    for axis, size in (("row", rows), ("col", cols)):
-        chi = sum([swapped(chi, axis, step) for step in range(size)])
+    copies = jnp.broadcast_to(chi[None], (rows * cols, *chi.shape))
+    copies = lax.all_to_all(copies, ("row", "col"), split_axis=0, concat_axis=0, tiled=True)
+    chi = copies.sum(axis=0)
     return chi / NAO
 
 

time: 879 us -> 849 us (0.966)
  waiting for transfers between devices: 573 us -> 537 us
  blocking collectives: 0 us -> 12.3 us
    all_to_all x5, waiting for transfers between devices: 158 us -> 93 us  [along_row(): return lax.all_to_all(value, 'row', split_axis=0, concat_axis=0, tiled=True)]
    all_gather x1, waiting for transfers between devices: 45.2 us -> 69.4 us  [shards(): whole = lax.all_gather(whole, 'row', axis=0, tiled=False)]
    all_to_all x0 -> x1, blocking collectives: none -> 12.3 us  [shards(): lax.all_to_all(copies, ('row', 'col'), split_axis=0, concat_axis=0, tiled...]
    ppermute x25 -> x19, waiting for transfers between devices: 293 us -> 299 us  [swapped(): return lax.ppermute(value, axis, pairs)]
    ppermute x25 -> x19, starting transfers between devices: 27.7 us -> 22.1 us  [swapped(): return lax.ppermute(value, axis, pairs)]
  transfers between devices with their start and end apart: 32 -> 26, of which waited for: 19 -> 18; matrix products, arithmetic and copies ran while one was open for 0% -> 0% of each run, Pallas kernels for 23% -> 24%
where the time goes in v1:
time: 849 us; the launch traced here: 848 us
  waiting for transfers between devices  537 us (63%)
  Pallas kernels  227 us (27%)
  starting transfers between devices  51.3 us (6%)
  between operations  13.6 us (2%)
  blocking collectives  12.3 us (1%)
    ppermute x19, waiting for transfers between devices, swapped(): return lax.ppermute(value, axis, pairs)  299 us
    all_to_all x5, waiting for transfers between devices, along_row(): return lax.all_to_all(value, 'row', split_axis=0, concat_axis=0, tiled=True)  93 us
    all_gather x1, waiting for transfers between devices, shards(): whole = lax.all_gather(whole, ('col', 'aux'), axis=0, tiled=False)  75.3 us
    all_gather x1, waiting for transfers between devices, shards(): whole = lax.all_gather(whole, 'row', axis=0, tiled=False)  69.4 us
    pallas_call x4, Pallas kernels, fully_transformed(): pl.pallas_call(body, grid=(1,), in_specs=[alone((nao, nao), (0, 0))] + [a...  62.3 us
    pallas_call x4, Pallas kernels, half_transformed(): pl.pallas_call(body, grid=(1,), in_specs=[pl.BlockSpec((nao, nao), lambda...  59.9 us
    pallas_call x3, Pallas kernels, contracted(): pl.pallas_call(body, grid=(jpart // tall,), in_specs=[pl.BlockSpec((rows,...  40.7 us
    all_to_all x5, starting transfers between devices, along_row(): return lax.all_to_all(value, 'row', split_axis=0, concat_axis=0, tiled=True)  29.1 us
  transfers between devices with their start and end apart: 26, of which 18 were waited for; matrix products, arithmetic and copies ran while one was open for 0% of the time, Pallas kernels for 24%

profile of v1, /device:TPU:0, one launch (start us, length us, event | category | flops | bytes accessed | tf_op | source)
XLA Modules:
  0.0 847.9 jit_solution(3640218933449610760)
XLA Ops:
  13.2 6.4 all-to-all-start
  19.5 8.3 masked_piece.4.refs_2_.refs_0_
  27.8 69.4 %all-gather.5.cloned.1.call-done = bf16[8,64,2048]{2,1,0:T(8,128)(2,1)} async-done(((bf16[2,64,2048]{2,1,0:T(8,128)(2,1)}), bf16[8,64,2048]{2,1,0:T(8,128)(2,1)}) %all-gather.5.cloned.1.call-update) | async-done | bytes 2097168 | tf_op jit(solution)/shard_map/all_gather | solution.py:368
  108.4 8.1 masked_piece.5.refs_0_
  116.6 75.3 %all-gather.7.cloned.1.call-done = bf16[32,2,64,2048]{3,2,1,0:T(8,128)(2,1)} async-done(((bf16[4,2,64,2048]{3,2,1,0:T(8,128)(2,1)}), bf16[32,2,64,2048]{3,2,1,0:T(8,128)(2,1)}) %all-gather.7.cloned.1.call-update) | async-done | bytes 16777232 | tf_op jit(solution)/shard_map/all_gather | solution.py:370
  191.9 14.1 %occupied_order.1 = bf16[4,4,128,2048]{3,2,1,0:T(8,128)(2,1)} custom-call(s32[4]{0:T(128)S(1)} %iota_xor_fusion.order_ref, bf16[8,4,2,64,2048]{4,3,2,1,0:T(8,128)(2,1)} %bitcast.21, bf16[4,3,512,512]{3,2,1,0:T(8,128)(2,1)} %masked_piece.5.refs_0_), custom_call_target="tpu_custom_call" | custom-call | bytes 16777216 | tf_op jit(solution)/shard_map/occupied_order/pallas_call | solution.py:140
  206.0 12.7 %virtual_order.1.refs_0_.virt_ref = bf16[2048,2048]{1,0:T(8,128)(2,1)} custom-call(s32[4]{0:T(128)S(1)} %iota_xor_fusion.order_ref, bf16[8,4,2,64,2048]{4,3,2,1,0:T(8,128)(2,1)} %bitcast.22, bf16[2048,2048]{1,0:T(8,128)(2,1)} %bitcast.16), custom_call_target="tpu_custom_call" | custom-call | bytes 16777216 | tf_op jit(solution)/shard_map/virtual_order/pallas_call | solution.py:167
  218.7 9.0 %half_transformed.4 = (bf16[1,512,512]{2,1,0:T(8,128)(2,1)S(1)}, bf16[1,512,512]{2,1,0:T(8,128)(2,1)S(1)}, bf16[1,512,512]{2,1,0:T(8,128)(2,1)S(1)}, bf16[1,512,512]{2,1,0:T(8,128)(2,1)S(1)}) custom-call(bf16[2048,2048]{1,0:T(8,128)(2,1)} %bitcast.17, bf16[4,1,512,512]{3,2,1,0:T(8,128)(2,1)S(1)} %copy-done.1, bf16[2048,2048]{1,0:T(8,128)(2,1)} %virtual_order.1.refs_0_.virt_ref), custom_call_target="tpu_custom_call" | custom-call | flops 4294967296 | bytes 12582912 | tf_op jit(solution)/shard_map/half_transformed/pallas_call | solution.py:268
  231.3 11.3 %collective-permute-done.refs_1_ = bf16[1,512,512]{2,1,0:T(8,128)(2,1)S(1)} collective-permute-done((bf16[1,512,512]{2,1,0:T(8,128)(2,1)S(1)}, bf16[1,512,512]{2,1,0:T(8,128)(2,1)S(1)}, u32[]{:S(2)}, u32[]{:S(2)}) %collective-permute-start) | collective-permute-done | bytes 524320 | tf_op jit(solution)/shard_map/ppermute | solution.py:21
  242.6 11.8 %collective-permute-done.1.refs_2_ = bf16[1,512,512]{2,1,0:T(8,128)(2,1)S(1)} collective-permute-done((bf16[1,512,512]{2,1,0:T(8,128)(2,1)S(1)}, bf16[1,512,512]{2,1,0:T(8,128)(2,1)S(1)}, u32[]{:S(2)}, u32[]{:S(2)}) %collective-permute-start.1) | collective-permute-done | bytes 524320 | tf_op jit(solution)/shard_map/ppermute | solution.py:21
  254.3 10.5 %fully_transformed.4.refs_2_.refs_4_ = bf16[4,5,128,2048]{3,2,1,0:T(8,128)(2,1)} custom-call(bf16[2048,2048]{1,0:T(8,128)(2,1)} %virtual_order.1.refs_0_.virt_ref, bf16[1,512,512]{2,1,0:T(8,128)(2,1)S(1)} %get-tuple-element.24.refs_0_.refs_4_, bf16[1,512,512]{2,1,0:T(8,128)(2,1)S(1)} %collective-permute-done.refs_1_, ...), custom_call_target="tpu_custom_call" | custom-call | flops 4294967296 | bytes 12582912 | tf_op jit(solution)/shard_map/fully_transformed/pallas_call | solution.py:317
  264.8 26.2 %all-to-all-done.1.refs_1_.moved_ref = bf16[4,4,512,512]{3,2,1,0:T(8,128)(2,1)} async-done(((bf16[4,4,512,512]{3,2,1,0:T(8,128)(2,1)}), bf16[4,4,512,512]{3,2,1,0:T(8,128)(2,1)}, u32[]{:S(2)}, u32[]{:S(2)}) %all-to-all-start.1) | async-done | bytes 8388640 | tf_op jit(solution)/shard_map/all_to_all | solution.py:351
  296.4 15.0 %half_transformed.5 = (bf16[2,512,512]{2,1,0:T(8,128)(2,1)S(1)}, bf16[2,512,512]{2,1,0:T(8,128)(2,1)S(1)}, bf16[2,512,512]{2,1,0:T(8,128)(2,1)S(1)}, bf16[2,512,512]{2,1,0:T(8,128)(2,1)S(1)}) custom-call(bf16[2048,2048]{1,0:T(8,128)(2,1)} %bitcast.18, bf16[4,4,512,512]{3,2,1,0:T(8,128)(2,1)} %all-to-all-done.1.refs_1_.moved_ref, ...), custom_call_target="tpu_custom_call" | custom-call | flops 8589934592 | bytes 16777216 | tf_op jit(solution)/shard_map/half_transformed/pallas_call | solution.py:268
  315.0 14.8 %half_transformed.6 = (bf16[2,512,512]{2,1,0:T(8,128)(2,1)S(1)}, bf16[2,512,512]{2,1,0:T(8,128)(2,1)S(1)}, bf16[2,512,512]{2,1,0:T(8,128)(2,1)S(1)}, bf16[2,512,512]{2,1,0:T(8,128)(2,1)S(1)}) custom-call(bf16[2048,2048]{1,0:T(8,128)(2,1)} %bitcast.19, bf16[4,4,512,512]{3,2,1,0:T(8,128)(2,1)} %all-to-all-done.1.refs_1_.moved_ref, ...), custom_call_target="tpu_custom_call" | custom-call | flops 8589934592 | bytes 16777216 | tf_op jit(solution)/shard_map/half_transformed/pallas_call | solution.py:268
  340.0 21.5 %collective-permute-done.7.refs_2_ = bf16[2,512,512]{2,1,0:T(8,128)(2,1)S(1)} collective-permute-done((bf16[2,512,512]{2,1,0:T(8,128)(2,1)S(1)}, bf16[2,512,512]{2,1,0:T(8,128)(2,1)S(1)}, u32[]{:S(2)}, u32[]{:S(2)}) %collective-permute-start.7) | collective-permute-done | bytes 1048608 | tf_op jit(solution)/shard_map/ppermute | solution.py:21
  361.5 15.4 %fully_transformed.5.refs_4_ = bf16[4,5,128,2048]{3,2,1,0:T(8,128)(2,1)} custom-call(bf16[2048,2048]{1,0:T(8,128)(2,1)} %virtual_order.1.refs_0_.virt_ref, bf16[2,512,512]{2,1,0:T(8,128)(2,1)S(1)} %get-tuple-element.28.refs_0_, bf16[2,512,512]{2,1,0:T(8,128)(2,1)S(1)} %collective-permute-done.6.refs_1_, ...), custom_call_target="tpu_custom_call", output_to_operand_aliasing={{}: (5, {})} | custom-call | flops 8589934592 | bytes 16777216 | tf_op jit(solution)/shard_map/fully_transformed/pallas_call | solution.py:317
  382.6 21.7 %collective-permute-done.4.refs_2_ = bf16[2,512,512]{2,1,0:T(8,128)(2,1)S(1)} collective-permute-done((bf16[2,512,512]{2,1,0:T(8,128)(2,1)S(1)}, bf16[2,512,512]{2,1,0:T(8,128)(2,1)S(1)}, u32[]{:S(2)}, u32[]{:S(2)}) %collective-permute-start.4) | collective-permute-done | bytes 1048608 | tf_op jit(solution)/shard_map/ppermute | solution.py:21
  404.2 15.4 %fully_transformed.6.refs_3_.refs_0_ = bf16[4,5,128,2048]{3,2,1,0:T(8,128)(2,1)} custom-call(bf16[2048,2048]{1,0:T(8,128)(2,1)} %virtual_order.1.refs_0_.virt_ref, bf16[2,512,512]{2,1,0:T(8,128)(2,1)S(1)} %get-tuple-element.29.refs_5_.refs_0_, bf16[2,512,512]{2,1,0:T(8,128)(2,1)S(1)} %collective-permute-done.3.refs_1_, ...), custom_call_target="tpu_custom_call", output_to_operand_aliasing={{}: (5, {})} | custom-call | flops 8589934592 | bytes 16777216 | tf_op jit(solution)/shard_map/fully_transformed/pallas_call | solution.py:317
  419.6 14.3 %all-to-all-done.3.moved_ref = bf16[4,3,512,512]{3,2,1,0:T(8,128)(2,1)} async-done(((bf16[4,3,512,512]{3,2,1,0:T(8,128)(2,1)}), bf16[4,3,512,512]{3,2,1,0:T(8,128)(2,1)}, u32[]{:S(2)}, u32[]{:S(2)}) %all-to-all-start.3) | async-done | bytes 6291488 | tf_op jit(solution)/shard_map/all_to_all | solution.py:351
  440.1 10.6 %masked_strips.2 = (bf16[32,128,512]{2,1,0:T(8,128)(2,1)}, bf16[32,128,512]{2,1,0:T(8,128)(2,1)}, bf16[32,128,512]{2,1,0:T(8,128)(2,1)}) custom-call(s32[3]{0:T(128)S(1)} %bitcast.12, s32[4,4]{1,0:T(4,128)S(1)} %dynamic_slice.3.tiles_ref, bf16[32,512,512]{2,1,0:T(8,128)(2,1)} %refs_0_.5, bf16[32,512,512]{2,1,0:T(8,128)(2,1)} %refs_0_.5, ...), custom_call_target="tpu_custom_call" | custom-call | bytes 25165824 | tf_op jit(solution)/shard_map/masked_strips/pallas_call | solution.py:113
  453.8 21.1 %half_transformed.7 = (bf16[3,512,512]{2,1,0:T(8,128)(2,1)S(1)}, bf16[3,512,512]{2,1,0:T(8,128)(2,1)S(1)}, bf16[3,512,512]{2,1,0:T(8,128)(2,1)S(1)}, bf16[3,512,512]{2,1,0:T(8,128)(2,1)}) custom-call(bf16[2048,2048]{1,0:T(8,128)(2,1)} %bitcast.20, bf16[4,3,512,512]{3,2,1,0:T(8,128)(2,1)} %all-to-all-done.3.moved_ref, ...), custom_call_target="tpu_custom_call" | custom-call | flops 12884901888 | bytes 20971520 | tf_op jit(solution)/shard_map/half_transformed/pallas_call | solution.py:268
  478.3 66.2 %collective-permute-done.10.refs_6_.refs_2_ = bf16[32,128,512]{2,1,0:T(8,128)(2,1)} collective-permute-done((bf16[32,128,512]{2,1,0:T(8,128)(2,1)}, bf16[32,128,512]{2,1,0:T(8,128)(2,1)}, u32[]{:S(2)}, u32[]{:S(2)}) %collective-permute-start.10) | collective-permute-done | bytes 4194336 | tf_op jit(solution)/shard_map/ppermute | solution.py:21
  546.1 33.6 %collective-permute-done.14.refs_1_ = bf16[3,512,512]{2,1,0:T(8,128)(2,1)S(1)} collective-permute-done((bf16[3,512,512]{2,1,0:T(8,128)(2,1)S(1)}, bf16[3,512,512]{2,1,0:T(8,128)(2,1)S(1)}, u32[]{:S(2)}, u32[]{:S(2)}) %collective-permute-start.14) | collective-permute-done | bytes 1572896 | tf_op jit(solution)/shard_map/ppermute | solution.py:21
  579.7 31.4 %collective-permute-done.16.refs_3_ = bf16[3,512,512]{2,1,0:T(8,128)(2,1)S(1)} collective-permute-done((bf16[3,512,512]{2,1,0:T(8,128)(2,1)}, bf16[3,512,512]{2,1,0:T(8,128)(2,1)S(1)}, u32[]{:S(2)}, u32[]{:S(2)}) %collective-permute-start.16) | collective-permute-done | bytes 1572896 | tf_op jit(solution)/shard_map/ppermute | solution.py:21
  612.3 21.0 %fully_transformed.7.refs_6_.refs_1_.refs_2_.refs_8_ = bf16[4,3,128,2048]{3,2,1,0:T(8,128)(2,1)} custom-call(bf16[2048,2048]{1,0:T(8,128)(2,1)} %virtual_order.1.refs_0_.virt_ref, bf16[3,512,512]{2,1,0:T(8,128)(2,1)S(1)} %get-tuple-element.39.refs_0_.refs_4_, bf16[3,512,512]{2,1,0:T(8,128)(2,1)S(1)} %collective-permute-done.14.refs_1_, ...), custom_call_target="tpu_custom_call" | custom-call | flops 12884901888 | bytes 20971520 | tf_op jit(solution)/shard_map/fully_transformed/pallas_call | solution.py:317
  633.3 34.1 %all-to-all-done.2.returned_ref = bf16[4,5,128,2048]{3,2,1,0:T(8,128)(2,1)} async-done(((bf16[4,5,128,2048]{3,2,1,0:T(8,128)(2,1)}), bf16[4,5,128,2048]{3,2,1,0:T(8,128)(2,1)}, u32[]{:S(2)}, u32[]{:S(2)}) %all-to-all-start.2) | async-done | bytes 10485792 | tf_op jit(solution)/shard_map/all_to_all | solution.py:351
  681.1 89.6 %collective-permute-done.17.refs_0_.refs_3_ = bf16[32,128,512]{2,1,0:T(8,128)(2,1)} collective-permute-done((bf16[32,128,512]{2,1,0:T(8,128)(2,1)S(1)}, bf16[32,128,512]{2,1,0:T(8,128)(2,1)}, u32[]{:S(2)}, u32[]{:S(2)}) %collective-permute-start.17) | collective-permute-done | bytes 4194336 | tf_op jit(solution)/shard_map/ppermute | solution.py:21
  770.7 17.5 %contracted.3 = f32[2,32,320]{2,1,0:T(8,128)S(1)} custom-call(bf16[4,5,128,2048]{3,2,1,0:T(8,128)(2,1)} %all-to-all-done.2.returned_ref, bf16[32,128,512]{2,1,0:T(8,128)(2,1)} %get-tuple-element.36.refs_0_, bf16[32,128,512]{2,1,0:T(8,128)(2,1)} %collective-permute-done.9.refs_5_.refs_1_, bf16[32,128,512]{2,1,0:T(8,128)(2,1)} %collective-permute-done.10.refs_6_.refs_2_, ...), custom_call_target="tpu_custom_call" | custom-call | flops 8053063680 | bytes 33030144 | tf_op jit(solution)/shard_map/contracted/pallas_call | solution.py:229
  788.4 7.5 contracted.4
  796.1 14.1 %all-to-all-done.4.returned_ref = bf16[4,3,128,2048]{3,2,1,0:T(8,128)(2,1)} async-done(((bf16[4,3,128,2048]{3,2,1,0:T(8,128)(2,1)}), bf16[4,3,128,2048]{3,2,1,0:T(8,128)(2,1)}, u32[]{:S(2)}, u32[]{:S(2)}) %all-to-all-start.4) | async-done | bytes 6291488 | tf_op jit(solution)/shard_map/all_to_all | solution.py:351
  810.3 15.8 %contracted.5 = f32[2,32,192]{2,1,0:T(8,128)S(1)} custom-call(bf16[4,3,128,2048]{3,2,1,0:T(8,128)(2,1)} %all-to-all-done.4.returned_ref, bf16[32,128,512]{2,1,0:T(8,128)(2,1)} %get-tuple-element.36.refs_0_, bf16[32,128,512]{2,1,0:T(8,128)(2,1)} %collective-permute-done.9.refs_5_.refs_1_, bf16[32,128,512]{2,1,0:T(8,128)(2,1)} %collective-permute-done.10.refs_6_.refs_2_, ...), custom_call_target="tpu_custom_call" | custom-call | flops 6442450944 | bytes 39845888 | tf_op jit(solution)/shard_map/contracted/pallas_call | solution.py:229
  826.6 12.3 %all_to_all.30 = f32[16,1,2048]{2,1,0:T(1,128)S(1)} all-to-all(f32[16,1,2048]{2,1,0:T(1,128)S(1)} %reshape.27), channel_id=1, replica_groups=mesh['aux'=2,'row'=4,'col'=4] {'row','col'}, dimensions={0} | all-to-all | bytes 262144 | tf_op jit(solution)/shard_map/all_to_all | solution.py:412
  (71 shorter events, 78.5 us)
Async XLA Ops:
  6.5 90.6 %all-gather.5.cloned.1.call-start = ((), (), s32[]{:S(2)}) async-start(), calls=%async_computation.6 | async-start | bytes 2621440 | tf_op jit(solution)/shard_map/all_gather | solution.py:368
  13.2 88.2 %all-to-all-start = ((bf16[4,1,512,512]{3,2,1,0:T(8,128)(2,1)}), bf16[4,1,512,512]{3,2,1,0:T(8,128)(2,1)S(1)}, u32[]{:S(2)}, u32[]{:S(2)}) async-start(bf16[4,1,512,512]{3,2,1,0:T(8,128)(2,1)} %masked_piece.3.refs_2_.refs_0_), calls=%async_computation | async-start | bytes 4194304 | tf_op jit(solution)/shard_map/all_to_all | solution.py:351
  19.5 172.4 %all-gather.7.cloned.1.call-start = ((), (), s32[]{:S(2)}) async-start(), calls=%async_computation.7 | async-start | bytes 18874368 | tf_op jit(solution)/shard_map/all_gather | solution.py:370
  101.4 1.3 copy-start
  102.8 188.2 %all-to-all-start.1 = ((bf16[4,4,512,512]{3,2,1,0:T(8,128)(2,1)}), bf16[4,4,512,512]{3,2,1,0:T(8,128)(2,1)}, u32[]{:S(2)}, u32[]{:S(2)}) async-start(bf16[4,4,512,512]{3,2,1,0:T(8,128)(2,1)} %masked_piece.4.refs_2_.refs_0_), calls=%async_computation.1 | async-start | bytes 16777216 | tf_op jit(solution)/shard_map/all_to_all | solution.py:351
  206.0 12.7 %copy-start.1 = (bf16[4,1,512,512]{3,2,1,0:T(8,128)(2,1)S(1)}, bf16[4,1,512,512]{3,2,1,0:T(8,128)(2,1)}, u32[]{:S(2)}) copy-start(bf16[4,1,512,512]{3,2,1,0:T(8,128)(2,1)} %copy-done) | copy-start | bytes 6291460
  227.7 14.8 %collective-permute-start = (bf16[1,512,512]{2,1,0:T(8,128)(2,1)S(1)}, bf16[1,512,512]{2,1,0:T(8,128)(2,1)S(1)}, u32[]{:S(2)}, u32[]{:S(2)}) collective-permute-start(bf16[1,512,512]{2,1,0:T(8,128)(2,1)S(1)} %get-tuple-element.25), channel_id=1, source_target_pairs={{0,1},{1,0},{2,3},{3,2},{4,5},{5,4},{6,7},{7,6},{8,9},{9,8},{10,11... | collective-permute-start | bytes 1572872 | tf_op jit(solution)/shard_map/ppermute | solution.py:21
  229.3 25.0 %collective-permute-start.1 = (bf16[1,512,512]{2,1,0:T(8,128)(2,1)S(1)}, bf16[1,512,512]{2,1,0:T(8,128)(2,1)S(1)}, u32[]{:S(2)}, u32[]{:S(2)}) collective-permute-start(bf16[1,512,512]{2,1,0:T(8,128)(2,1)S(1)} %get-tuple-element.26), channel_id=1, source_target_pairs={{0,2},{1,3},{2,0},{3,1},{4,6},{5,7},{6,4},{7,5},{8,10},{9,11},{10,... | collective-permute-start | bytes 1572872 | tf_op jit(solution)/shard_map/ppermute | solution.py:21
  229.8 24.5 %collective-permute-start.2 = (bf16[1,512,512]{2,1,0:T(8,128)(2,1)S(1)}, bf16[1,512,512]{2,1,0:T(8,128)(2,1)S(1)}, u32[]{:S(2)}, u32[]{:S(2)}) collective-permute-start(bf16[1,512,512]{2,1,0:T(8,128)(2,1)S(1)} %get-tuple-element.27), channel_id=1, source_target_pairs={{0,3},{1,2},{2,1},{3,0},{4,7},{5,6},{6,5},{7,4},{8,11},{9,10},{10,... | collective-permute-start | bytes 1572872 | tf_op jit(solution)/shard_map/ppermute | solution.py:21
  291.0 142.9 %all-to-all-start.3 = ((bf16[4,3,512,512]{3,2,1,0:T(8,128)(2,1)}), bf16[4,3,512,512]{3,2,1,0:T(8,128)(2,1)}, u32[]{:S(2)}, u32[]{:S(2)}) async-start(bf16[4,3,512,512]{3,2,1,0:T(8,128)(2,1)} %ordered.3.refs_0_), calls=%async_computation.3 | async-start | bytes 12582912 | tf_op jit(solution)/shard_map/all_to_all | solution.py:351
  311.4 26.2 %collective-permute-start.6 = (bf16[2,512,512]{2,1,0:T(8,128)(2,1)S(1)}, bf16[2,512,512]{2,1,0:T(8,128)(2,1)S(1)}, u32[]{:S(2)}, u32[]{:S(2)}) collective-permute-start(bf16[2,512,512]{2,1,0:T(8,128)(2,1)S(1)} %get-tuple-element.33), channel_id=1, source_target_pairs={{0,1},{1,0},{2,3},{3,2},{4,5},{5,4},{6,7},{7,6},{8,9},{9,8},{10,11... | collective-permute-start | bytes 3145736 | tf_op jit(solution)/shard_map/ppermute | solution.py:21
  313.0 48.6 %collective-permute-start.7 = (bf16[2,512,512]{2,1,0:T(8,128)(2,1)S(1)}, bf16[2,512,512]{2,1,0:T(8,128)(2,1)S(1)}, u32[]{:S(2)}, u32[]{:S(2)}) collective-permute-start(bf16[2,512,512]{2,1,0:T(8,128)(2,1)S(1)} %get-tuple-element.34), channel_id=1, source_target_pairs={{0,2},{1,3},{2,0},{3,1},{4,6},{5,7},{6,4},{7,5},{8,10},{9,11},{10,... | collective-permute-start | bytes 3145736 | tf_op jit(solution)/shard_map/ppermute | solution.py:21
  314.5 47.0 %collective-permute-start.8 = (bf16[2,512,512]{2,1,0:T(8,128)(2,1)S(1)}, bf16[2,512,512]{2,1,0:T(8,128)(2,1)S(1)}, u32[]{:S(2)}, u32[]{:S(2)}) collective-permute-start(bf16[2,512,512]{2,1,0:T(8,128)(2,1)S(1)} %get-tuple-element.35), channel_id=1, source_target_pairs={{0,3},{1,2},{2,1},{3,0},{4,7},{5,6},{6,5},{7,4},{8,11},{9,10},{10,... | collective-permute-start | bytes 3145736 | tf_op jit(solution)/shard_map/ppermute | solution.py:21
  329.8 52.7 %collective-permute-start.3 = (bf16[2,512,512]{2,1,0:T(8,128)(2,1)S(1)}, bf16[2,512,512]{2,1,0:T(8,128)(2,1)S(1)}, u32[]{:S(2)}, u32[]{:S(2)}) collective-permute-start(bf16[2,512,512]{2,1,0:T(8,128)(2,1)S(1)} %get-tuple-element.30), channel_id=1, source_target_pairs={{0,1},{1,0},{2,3},{3,2},{4,5},{5,4},{6,7},{7,6},{8,9},{9,8},{10,11... | collective-permute-start | bytes 3145736 | tf_op jit(solution)/shard_map/ppermute | solution.py:21
  331.3 72.9 %collective-permute-start.4 = (bf16[2,512,512]{2,1,0:T(8,128)(2,1)S(1)}, bf16[2,512,512]{2,1,0:T(8,128)(2,1)S(1)}, u32[]{:S(2)}, u32[]{:S(2)}) collective-permute-start(bf16[2,512,512]{2,1,0:T(8,128)(2,1)S(1)} %get-tuple-element.31), channel_id=1, source_target_pairs={{0,2},{1,3},{2,0},{3,1},{4,6},{5,7},{6,4},{7,5},{8,10},{9,11},{10,... | collective-permute-start | bytes 3145736 | tf_op jit(solution)/shard_map/ppermute | solution.py:21
  337.6 66.6 %collective-permute-start.5 = (bf16[2,512,512]{2,1,0:T(8,128)(2,1)S(1)}, bf16[2,512,512]{2,1,0:T(8,128)(2,1)S(1)}, u32[]{:S(2)}, u32[]{:S(2)}) collective-permute-start(bf16[2,512,512]{2,1,0:T(8,128)(2,1)S(1)} %get-tuple-element.32), channel_id=1, source_target_pairs={{0,3},{1,2},{2,1},{3,0},{4,7},{5,6},{6,5},{7,4},{8,11},{9,10},{10,... | collective-permute-start | bytes 3145736 | tf_op jit(solution)/shard_map/ppermute | solution.py:21
  433.9 233.5 %all-to-all-start.2 = ((bf16[4,5,128,2048]{3,2,1,0:T(8,128)(2,1)}), bf16[4,5,128,2048]{3,2,1,0:T(8,128)(2,1)}, u32[]{:S(2)}, u32[]{:S(2)}) async-start(bf16[4,5,128,2048]{3,2,1,0:T(8,128)(2,1)} %fully_transformed.6.refs_3_.refs_0_), calls=%async_computation.2 | async-start | bytes 20971520 | tf_op jit(solution)/shard_map/all_to_all | solution.py:351
  450.8 93.8 %collective-permute-start.10 = (bf16[32,128,512]{2,1,0:T(8,128)(2,1)}, bf16[32,128,512]{2,1,0:T(8,128)(2,1)}, u32[]{:S(2)}, u32[]{:S(2)}) collective-permute-start(bf16[32,128,512]{2,1,0:T(8,128)(2,1)} %get-tuple-element.38), channel_id=1, source_target_pairs={{0,2},{1,3},{2,0},{3,1},{4,6},{5,7},{6,4},{7,5},{8,10},{9,11},{10,... | collective-permute-start | bytes 12582920 | tf_op jit(solution)/shard_map/ppermute | solution.py:21
  452.3 93.8 %collective-permute-start.9 = (bf16[32,128,512]{2,1,0:T(8,128)(2,1)}, bf16[32,128,512]{2,1,0:T(8,128)(2,1)}, u32[]{:S(2)}, u32[]{:S(2)}) collective-permute-start(bf16[32,128,512]{2,1,0:T(8,128)(2,1)} %get-tuple-element.37), channel_id=1, source_target_pairs={{0,1},{1,0},{2,3},{3,2},{4,5},{5,4},{6,7},{7,6},{8,9},{9,8},{10,11... | collective-permute-start | bytes 12582920 | tf_op jit(solution)/shard_map/ppermute | solution.py:21
  474.8 104.9 %collective-permute-start.14 = (bf16[3,512,512]{2,1,0:T(8,128)(2,1)S(1)}, bf16[3,512,512]{2,1,0:T(8,128)(2,1)S(1)}, u32[]{:S(2)}, u32[]{:S(2)}) collective-permute-start(bf16[3,512,512]{2,1,0:T(8,128)(2,1)S(1)} %get-tuple-element.40), channel_id=1, source_target_pairs={{0,1},{1,0},{2,3},{3,2},{4,5},{5,4},{6,7},{7,6},{8,9},{9,8},{10,11... | collective-permute-start | bytes 4718600 | tf_op jit(solution)/shard_map/ppermute | solution.py:21
  475.4 104.3 %collective-permute-start.15 = (bf16[3,512,512]{2,1,0:T(8,128)(2,1)S(1)}, bf16[3,512,512]{2,1,0:T(8,128)(2,1)S(1)}, u32[]{:S(2)}, u32[]{:S(2)}) collective-permute-start(bf16[3,512,512]{2,1,0:T(8,128)(2,1)S(1)} %get-tuple-element.41), channel_id=1, source_target_pairs={{0,2},{1,3},{2,0},{3,1},{4,6},{5,7},{6,4},{7,5},{8,10},{9,11},{10,... | collective-permute-start | bytes 4718600 | tf_op jit(solution)/shard_map/ppermute | solution.py:21
  475.9 135.2 %collective-permute-start.16 = (bf16[3,512,512]{2,1,0:T(8,128)(2,1)}, bf16[3,512,512]{2,1,0:T(8,128)(2,1)S(1)}, u32[]{:S(2)}, u32[]{:S(2)}) collective-permute-start(bf16[3,512,512]{2,1,0:T(8,128)(2,1)} %get-tuple-element.42), channel_id=1, source_target_pairs={{0,3},{1,2},{2,1},{3,0},{4,7},{5,6},{6,5},{7,4},{8,11},{9,10},{10,... | collective-permute-start | bytes 4718600 | tf_op jit(solution)/shard_map/ppermute | solution.py:21
  611.1 1.2 copy-start.2
  667.4 142.9 %all-to-all-start.4 = ((bf16[4,3,128,2048]{3,2,1,0:T(8,128)(2,1)}), bf16[4,3,128,2048]{3,2,1,0:T(8,128)(2,1)}, u32[]{:S(2)}, u32[]{:S(2)}) async-start(bf16[4,3,128,2048]{3,2,1,0:T(8,128)(2,1)} %fully_transformed.7.refs_6_.refs_1_.refs_2_.refs_8_), calls=%async_computation.4 | async-start | bytes 12582912 | tf_op jit(solution)/shard_map/all_to_all | solution.py:351
  678.0 92.6 %collective-permute-start.17 = (bf16[32,128,512]{2,1,0:T(8,128)(2,1)S(1)}, bf16[32,128,512]{2,1,0:T(8,128)(2,1)}, u32[]{:S(2)}, u32[]{:S(2)}) collective-permute-start(bf16[32,128,512]{2,1,0:T(8,128)(2,1)S(1)} %masked_strips.3), channel_id=1, source_target_pairs={{0,3},{1,2},{2,1},{3,0},{4,7},{5,6},{6,5},{7,4},{8,11},{9,10},{10,... | collective-permute-start | bytes 12582920 | tf_op jit(solution)/shard_map/ppermute | solution.py:21
  680.6 90.1 %collective-permute-start.11 = (bf16[32,128,512]{2,1,0:T(8,128)(2,1)}, bf16[32,128,512]{2,1,0:T(8,128)(2,1)}, u32[]{:S(2)}, u32[]{:S(2)}) collective-permute-start(bf16[32,128,512]{2,1,0:T(8,128)(2,1)} %get-tuple-element.36.refs_0_), channel_id=1, source_target_pairs={{0,16},{16,0},{1,17},{17,1},{2,18},{18,2},{3,19},{19,3},{4,20},{20... | collective-permute-start | bytes 12582920 | tf_op jit(solution)/shard_map/ppermute | solution.py:21
  680.6 90.1 %collective-permute-start.12 = (bf16[32,128,512]{2,1,0:T(8,128)(2,1)}, bf16[32,128,512]{2,1,0:T(8,128)(2,1)}, u32[]{:S(2)}, u32[]{:S(2)}) collective-permute-start(bf16[32,128,512]{2,1,0:T(8,128)(2,1)} %collective-permute-done.9.refs_5_.refs_1_), channel_id=1, source_target_pairs={{0,16},{16,0},{1,17},{17,1},{2,18},{18,2},{3,19},{19,3},{4,20},{20... | collective-permute-start | bytes 12582920 | tf_op jit(solution)/shard_map/ppermute | solution.py:21
  681.1 89.6 %collective-permute-start.13 = (bf16[32,128,512]{2,1,0:T(8,128)(2,1)}, bf16[32,128,512]{2,1,0:T(8,128)(2,1)}, u32[]{:S(2)}, u32[]{:S(2)}) collective-permute-start(bf16[32,128,512]{2,1,0:T(8,128)(2,1)} %collective-permute-done.10.refs_6_.refs_2_), channel_id=1, source_target_pairs={{0,16},{16,0},{1,17},{17,1},{2,18},{18,2},{3,19},{19,3},{4,20},{20... | collective-permute-start | bytes 12582920 | tf_op jit(solution)/shard_map/ppermute | solution.py:21
  770.6 17.7 %collective-permute-start.18 = (bf16[32,128,512]{2,1,0:T(8,128)(2,1)}, bf16[32,128,512]{2,1,0:T(8,128)(2,1)}, u32[]{:S(2)}, u32[]{:S(2)}) collective-permute-start(bf16[32,128,512]{2,1,0:T(8,128)(2,1)} %collective-permute-done.17.refs_0_.refs_3_), channel_id=1, source_target_pairs={{0,16},{16,0},{1,17},{17,1},{2,18},{18,2},{3,19},{19,3},{4,20},{20... | collective-permute-start | bytes 12582920 | tf_op jit(solution)/shard_map/ppermute | solution.py:21
Sparse Core Ops, SparseCore 0:
  13.3 83.8 all-gather.4
  102.9 88.9 all-gather.6

commit v2 on v1

--- a/solution.py
+++ b/solution.py
@@ -185,7 +185,33 @@
     )(order, whole, *after)
 
 
-def contracted(returned, strips, first, after):
+def held(arrays, after):
+    count = len(arrays)
+
+    def body(*refs):
+        ins, outs, sems = refs[:count], refs[count + len(after) : -1], refs[-1]
+        copies = [
+            pltpu.make_async_copy(source, target, sems.at[index])
+            for index, (source, target) in enumerate(zip(ins, outs))
+        ]
+        for copy in copies:
+            copy.start()
+        for copy in copies:
+            copy.wait()
+
+    return pl.pallas_call(
+        body,
+        in_specs=[ANY] * (count + len(after)),
+        out_specs=[WHOLE] * count,
+        out_shape=[jax.ShapeDtypeStruct(value.shape, value.dtype) for value in arrays],
+        scratch_shapes=[pltpu.SemaphoreType.DMA((count,))],
+        cost_estimate=cost(0, sum(4 * value.size for value in arrays)),
+        compiler_params=pltpu.CompilerParams(vmem_limit_bytes=24 * 2**20),
+        name="held",
+    )(*arrays, *after)
+
+
+def contracted(returned, strips, first, after, near=False):
     rows, per, jpart, nao = returned.shape
     pdev, _, ncol = strips[0][0].shape
     left = rows * per
@@ -213,8 +239,12 @@
             mine = returned_ref[:, :, here, begin : begin + steps * ncol]
             mine = mine.reshape(left * group, steps * ncol)
             for half in range(len(strips)):
+                spot = here
+                if near and half == 0:
+                    start = pl.program_id(0) * tall + lower
+                    spot = pl.ds(pl.multiple_of(start, group), group)
                 other = [
-                    ref[:, here, :].reshape(pdev * group, ncol)
+                    ref[:, spot, :].reshape(pdev * group, ncol)
                     for ref in ins[half * steps : (half + 1) * steps]
                 ]
                 total = lax.dot_general(
@@ -230,7 +260,8 @@
         body,
         grid=(jpart // tall,),
         in_specs=[pl.BlockSpec((rows, per, tall, width), lambda i: (0, 0, i, place))]
-        + [pl.BlockSpec((pdev, tall, ncol), lambda i: (0, i, 0))] * count
+        + [WHOLE if near else pl.BlockSpec((pdev, tall, ncol), lambda i: (0, i, 0))] * steps
+        + [pl.BlockSpec((pdev, tall, ncol), lambda i: (0, i, 0))] * (count - steps)
         + [ANY] * len(after),
         out_specs=pl.BlockSpec((len(strips), pdev, left * group), lambda i: (0, 0, 0)),
         out_shape=jax.ShapeDtypeStruct((len(strips), pdev, left * group), F32),
@@ -238,7 +269,7 @@
             2 * count * pdev * left * group * jpart * ncol,
             2 * jpart * ncol * (count * pdev + steps * left),
         ),
-        compiler_params=params(),
+        compiler_params=pltpu.CompilerParams(vmem_limit_bytes=(40 if near else 26) * 2**20),
         name="contracted",
     )(returned, *flat, *after)
     result = result.reshape(len(strips), pdev, rows, per, group).sum(axis=-1)
@@ -403,9 +434,9 @@
 
     parts = [
         contracted(back[0], [strips[:-1], theirs[:-1]], 0, [second])
-        + contracted(back[0], [strips[-1:], theirs[-1:]], cols - 1, [second]),
-        contracted(back[1], [strips, theirs], 0, [second]),
+        + contracted(back[0], [strips[-1:], theirs[-1:]], cols - 1, [second])
     ]
+    parts.append(contracted(back[1], [held(strips, parts), theirs], 0, [second], True))
     chi = jnp.concatenate(parts, axis=1)
     chi = jnp.where(aux_idx == 0, chi, chi[:, :, ::-1]).reshape(pdev, 2 * pdev)
     copies = jnp.broadcast_to(chi[None], (rows * cols, *chi.shape))

time: 849 us -> 859 us (1.012)
  local copies, waits for them, and re-layouts: 5.2 us -> 22.7 us
  waiting for transfers between devices: 537 us -> 522 us
    unnamed x8 -> x24, local copies, waits for them, and re-layouts: 2.81 us -> 20.2 us
    all_to_all x5, waiting for transfers between devices: 93 us -> 78.6 us  [along_row(): return lax.all_to_all(value, 'row', split_axis=0, concat_axis=0, tiled=True)]
  transfers between devices with their start and end apart: 26 -> 26, of which waited for: 18 -> 17; matrix products, arithmetic and copies ran while one was open for 0% -> 0% of each run, Pallas kernels for 24% -> 25%
where the time goes in v2:
time: 859 us; the launch traced here: 858 us
  waiting for transfers between devices  522 us (61%)
  Pallas kernels  232 us (27%)
  starting transfers between devices  51.3 us (6%)
  local copies, waits for them, and re-layouts  22.7 us (3%)
  blocking collectives  14.4 us (2%)
  between operations  13.7 us (2%)
    ppermute x19, waiting for transfers between devices, swapped(): return lax.ppermute(value, axis, pairs)  299 us
    all_to_all x5, waiting for transfers between devices, along_row(): return lax.all_to_all(value, 'row', split_axis=0, concat_axis=0, tiled=True)  78.6 us
    all_gather x1, waiting for transfers between devices, shards(): whole = lax.all_gather(whole, ('col', 'aux'), axis=0, tiled=False)  75.3 us
    all_gather x1, waiting for transfers between devices, shards(): whole = lax.all_gather(whole, 'row', axis=0, tiled=False)  69.4 us
    pallas_call x4, Pallas kernels, fully_transformed(): pl.pallas_call(body, grid=(1,), in_specs=[alone((nao, nao), (0, 0))] + [a...  62.4 us
    pallas_call x4, Pallas kernels, half_transformed(): pl.pallas_call(body, grid=(1,), in_specs=[pl.BlockSpec((nao, nao), lambda...  59.9 us
    pallas_call x3, Pallas kernels, contracted(): pl.pallas_call(body, grid=(jpart // tall,), in_specs=[pl.BlockSpec((rows,...  39.1 us
    all_to_all x5, starting transfers between devices, along_row(): return lax.all_to_all(value, 'row', split_axis=0, concat_axis=0, tiled=True)  29.1 us
  transfers between devices with their start and end apart: 26, of which 17 were waited for; matrix products, arithmetic and copies ran while one was open for 0% of the time, Pallas kernels for 25%

profile of v2, /device:TPU:0, one launch (start us, length us, event | category | flops | bytes accessed | tf_op | source)
XLA Modules:
  0.0 857.7 jit_solution(6620693159743184085)
XLA Ops:
  13.2 6.4 all-to-all-start
  19.5 8.3 masked_piece.4.refs_2_.refs_0_
  27.8 69.4 %all-gather.5.cloned.1.call-done = bf16[8,64,2048]{2,1,0:T(8,128)(2,1)} async-done(((bf16[2,64,2048]{2,1,0:T(8,128)(2,1)}), bf16[8,64,2048]{2,1,0:T(8,128)(2,1)}) %all-gather.5.cloned.1.call-update) | async-done | bytes 2097168 | tf_op jit(solution)/shard_map/all_gather | solution.py:399
  108.5 8.1 masked_piece.5.refs_0_
  116.6 75.3 %all-gather.7.cloned.1.call-done = bf16[32,2,64,2048]{3,2,1,0:T(8,128)(2,1)} async-done(((bf16[4,2,64,2048]{3,2,1,0:T(8,128)(2,1)}), bf16[32,2,64,2048]{3,2,1,0:T(8,128)(2,1)}) %all-gather.7.cloned.1.call-update) | async-done | bytes 16777232 | tf_op jit(solution)/shard_map/all_gather | solution.py:401
  191.9 14.2 %occupied_order.1 = bf16[4,4,128,2048]{3,2,1,0:T(8,128)(2,1)} custom-call(s32[4]{0:T(128)S(1)} %iota_xor_fusion.order_ref, bf16[8,4,2,64,2048]{4,3,2,1,0:T(8,128)(2,1)} %bitcast.27, bf16[4,3,512,512]{3,2,1,0:T(8,128)(2,1)} %masked_piece.5.refs_0_), custom_call_target="tpu_custom_call" | custom-call | bytes 16777216 | tf_op jit(solution)/shard_map/occupied_order/pallas_call | solution.py:140
  206.2 12.7 %virtual_order.1.refs_0_.virt_ref = bf16[2048,2048]{1,0:T(8,128)(2,1)} custom-call(s32[4]{0:T(128)S(1)} %iota_xor_fusion.order_ref, bf16[8,4,2,64,2048]{4,3,2,1,0:T(8,128)(2,1)} %bitcast.28, bf16[2048,2048]{1,0:T(8,128)(2,1)} %bitcast.22), custom_call_target="tpu_custom_call" | custom-call | bytes 16777216 | tf_op jit(solution)/shard_map/virtual_order/pallas_call | solution.py:167
  218.9 9.0 %half_transformed.4 = (bf16[1,512,512]{2,1,0:T(8,128)(2,1)S(1)}, bf16[1,512,512]{2,1,0:T(8,128)(2,1)S(1)}, bf16[1,512,512]{2,1,0:T(8,128)(2,1)S(1)}, bf16[1,512,512]{2,1,0:T(8,128)(2,1)S(1)}) custom-call(bf16[2048,2048]{1,0:T(8,128)(2,1)} %bitcast.23, bf16[4,1,512,512]{3,2,1,0:T(8,128)(2,1)S(1)} %copy-done.2, bf16[2048,2048]{1,0:T(8,128)(2,1)} %virtual_order.1.refs_0_.virt_ref), custom_call_target="tpu_custom_call" | custom-call | flops 4294967296 | bytes 12582912 | tf_op jit(solution)/shard_map/half_transformed/pallas_call | solution.py:299
  231.5 11.3 %collective-permute-done.refs_1_ = bf16[1,512,512]{2,1,0:T(8,128)(2,1)S(1)} collective-permute-done((bf16[1,512,512]{2,1,0:T(8,128)(2,1)S(1)}, bf16[1,512,512]{2,1,0:T(8,128)(2,1)S(1)}, u32[]{:S(2)}, u32[]{:S(2)}) %collective-permute-start) | collective-permute-done | bytes 524320 | tf_op jit(solution)/shard_map/ppermute | solution.py:21
  242.7 11.8 %collective-permute-done.1.refs_2_ = bf16[1,512,512]{2,1,0:T(8,128)(2,1)S(1)} collective-permute-done((bf16[1,512,512]{2,1,0:T(8,128)(2,1)S(1)}, bf16[1,512,512]{2,1,0:T(8,128)(2,1)S(1)}, u32[]{:S(2)}, u32[]{:S(2)}) %collective-permute-start.1) | collective-permute-done | bytes 524320 | tf_op jit(solution)/shard_map/ppermute | solution.py:21
  254.5 10.6 %fully_transformed.4.refs_2_.refs_4_ = bf16[4,5,128,2048]{3,2,1,0:T(8,128)(2,1)} custom-call(bf16[2048,2048]{1,0:T(8,128)(2,1)} %virtual_order.1.refs_0_.virt_ref, bf16[1,512,512]{2,1,0:T(8,128)(2,1)S(1)} %get-tuple-element.28.refs_0_.refs_4_, bf16[1,512,512]{2,1,0:T(8,128)(2,1)S(1)} %collective-permute-done.refs_1_, ...), custom_call_target="tpu_custom_call" | custom-call | flops 4294967296 | bytes 12582912 | tf_op jit(solution)/shard_map/fully_transformed/pallas_call | solution.py:348
  265.1 26.0 %all-to-all-done.1.refs_1_.moved_ref = bf16[4,4,512,512]{3,2,1,0:T(8,128)(2,1)} async-done(((bf16[4,4,512,512]{3,2,1,0:T(8,128)(2,1)}), bf16[4,4,512,512]{3,2,1,0:T(8,128)(2,1)}, u32[]{:S(2)}, u32[]{:S(2)}) %all-to-all-start.1) | async-done | bytes 8388640 | tf_op jit(solution)/shard_map/all_to_all | solution.py:382
  296.5 14.9 %half_transformed.5 = (bf16[2,512,512]{2,1,0:T(8,128)(2,1)S(1)}, bf16[2,512,512]{2,1,0:T(8,128)(2,1)S(1)}, bf16[2,512,512]{2,1,0:T(8,128)(2,1)S(1)}, bf16[2,512,512]{2,1,0:T(8,128)(2,1)S(1)}) custom-call(bf16[2048,2048]{1,0:T(8,128)(2,1)} %bitcast.24, bf16[4,4,512,512]{3,2,1,0:T(8,128)(2,1)} %all-to-all-done.1.refs_1_.moved_ref, ...), custom_call_target="tpu_custom_call" | custom-call | flops 8589934592 | bytes 16777216 | tf_op jit(solution)/shard_map/half_transformed/pallas_call | solution.py:299
  315.0 14.8 %half_transformed.6 = (bf16[2,512,512]{2,1,0:T(8,128)(2,1)S(1)}, bf16[2,512,512]{2,1,0:T(8,128)(2,1)S(1)}, bf16[2,512,512]{2,1,0:T(8,128)(2,1)S(1)}, bf16[2,512,512]{2,1,0:T(8,128)(2,1)S(1)}) custom-call(bf16[2048,2048]{1,0:T(8,128)(2,1)} %bitcast.25, bf16[4,4,512,512]{3,2,1,0:T(8,128)(2,1)} %all-to-all-done.1.refs_1_.moved_ref, ...), custom_call_target="tpu_custom_call" | custom-call | flops 8589934592 | bytes 16777216 | tf_op jit(solution)/shard_map/half_transformed/pallas_call | solution.py:299
  340.0 21.5 %collective-permute-done.7.refs_2_ = bf16[2,512,512]{2,1,0:T(8,128)(2,1)S(1)} collective-permute-done((bf16[2,512,512]{2,1,0:T(8,128)(2,1)S(1)}, bf16[2,512,512]{2,1,0:T(8,128)(2,1)S(1)}, u32[]{:S(2)}, u32[]{:S(2)}) %collective-permute-start.7) | collective-permute-done | bytes 1048608 | tf_op jit(solution)/shard_map/ppermute | solution.py:21
  361.5 15.4 %fully_transformed.5.refs_4_ = bf16[4,5,128,2048]{3,2,1,0:T(8,128)(2,1)} custom-call(bf16[2048,2048]{1,0:T(8,128)(2,1)} %virtual_order.1.refs_0_.virt_ref, bf16[2,512,512]{2,1,0:T(8,128)(2,1)S(1)} %get-tuple-element.32.refs_0_, bf16[2,512,512]{2,1,0:T(8,128)(2,1)S(1)} %collective-permute-done.6.refs_1_, ...), custom_call_target="tpu_custom_call", output_to_operand_aliasing={{}: (5, {})} | custom-call | flops 8589934592 | bytes 16777216 | tf_op jit(solution)/shard_map/fully_transformed/pallas_call | solution.py:348
  382.5 21.7 %collective-permute-done.4.refs_2_ = bf16[2,512,512]{2,1,0:T(8,128)(2,1)S(1)} collective-permute-done((bf16[2,512,512]{2,1,0:T(8,128)(2,1)S(1)}, bf16[2,512,512]{2,1,0:T(8,128)(2,1)S(1)}, u32[]{:S(2)}, u32[]{:S(2)}) %collective-permute-start.4) | collective-permute-done | bytes 1048608 | tf_op jit(solution)/shard_map/ppermute | solution.py:21
  404.2 15.4 %fully_transformed.6.refs_3_.refs_0_ = bf16[4,5,128,2048]{3,2,1,0:T(8,128)(2,1)} custom-call(bf16[2048,2048]{1,0:T(8,128)(2,1)} %virtual_order.1.refs_0_.virt_ref, bf16[2,512,512]{2,1,0:T(8,128)(2,1)S(1)} %get-tuple-element.33.refs_5_.refs_0_, bf16[2,512,512]{2,1,0:T(8,128)(2,1)S(1)} %collective-permute-done.3.refs_1_, ...), custom_call_target="tpu_custom_call", output_to_operand_aliasing={{}: (5, {})} | custom-call | flops 8589934592 | bytes 16777216 | tf_op jit(solution)/shard_map/fully_transformed/pallas_call | solution.py:348
  419.6 14.3 %all-to-all-done.3.moved_ref = bf16[4,3,512,512]{3,2,1,0:T(8,128)(2,1)} async-done(((bf16[4,3,512,512]{3,2,1,0:T(8,128)(2,1)}), bf16[4,3,512,512]{3,2,1,0:T(8,128)(2,1)}, u32[]{:S(2)}, u32[]{:S(2)}) %all-to-all-start.3) | async-done | bytes 6291488 | tf_op jit(solution)/shard_map/all_to_all | solution.py:382
  433.9 6.2 all-to-all-start.2
  440.1 10.6 %masked_strips.2 = (bf16[32,128,512]{2,1,0:T(8,128)(2,1)}, bf16[32,128,512]{2,1,0:T(8,128)(2,1)}, bf16[32,128,512]{2,1,0:T(8,128)(2,1)}) custom-call(s32[3]{0:T(128)S(1)} %bitcast.18, s32[4,4]{1,0:T(4,128)S(1)} %dynamic_slice.3.tiles_ref, bf16[32,512,512]{2,1,0:T(8,128)(2,1)} %refs_0_.5, bf16[32,512,512]{2,1,0:T(8,128)(2,1)} %refs_0_.5, ...), custom_call_target="tpu_custom_call" | custom-call | bytes 25165824 | tf_op jit(solution)/shard_map/masked_strips/pallas_call | solution.py:113
  453.8 21.1 %half_transformed.7 = (bf16[3,512,512]{2,1,0:T(8,128)(2,1)S(1)}, bf16[3,512,512]{2,1,0:T(8,128)(2,1)S(1)}, bf16[3,512,512]{2,1,0:T(8,128)(2,1)S(1)}, bf16[3,512,512]{2,1,0:T(8,128)(2,1)}) custom-call(bf16[2048,2048]{1,0:T(8,128)(2,1)} %bitcast.26, bf16[4,3,512,512]{3,2,1,0:T(8,128)(2,1)} %all-to-all-done.3.moved_ref, ...), custom_call_target="tpu_custom_call" | custom-call | flops 12884901888 | bytes 20971520 | tf_op jit(solution)/shard_map/half_transformed/pallas_call | solution.py:299
  478.3 66.2 %collective-permute-done.10.refs_6_.refs_2_ = bf16[32,128,512]{2,1,0:T(8,128)(2,1)} collective-permute-done((bf16[32,128,512]{2,1,0:T(8,128)(2,1)}, bf16[32,128,512]{2,1,0:T(8,128)(2,1)}, u32[]{:S(2)}, u32[]{:S(2)}) %collective-permute-start.10) | collective-permute-done | bytes 4194336 | tf_op jit(solution)/shard_map/ppermute | solution.py:21
  546.1 33.6 %collective-permute-done.14.refs_1_ = bf16[3,512,512]{2,1,0:T(8,128)(2,1)S(1)} collective-permute-done((bf16[3,512,512]{2,1,0:T(8,128)(2,1)S(1)}, bf16[3,512,512]{2,1,0:T(8,128)(2,1)S(1)}, u32[]{:S(2)}, u32[]{:S(2)}) %collective-permute-start.14) | collective-permute-done | bytes 1572896 | tf_op jit(solution)/shard_map/ppermute | solution.py:21
  579.7 31.4 %collective-permute-done.16.refs_3_ = bf16[3,512,512]{2,1,0:T(8,128)(2,1)S(1)} collective-permute-done((bf16[3,512,512]{2,1,0:T(8,128)(2,1)}, bf16[3,512,512]{2,1,0:T(8,128)(2,1)S(1)}, u32[]{:S(2)}, u32[]{:S(2)}) %collective-permute-start.16) | collective-permute-done | bytes 1572896 | tf_op jit(solution)/shard_map/ppermute | solution.py:21
  612.3 21.1 %fully_transformed.7.refs_6_.refs_1_.refs_2_.refs_8_ = bf16[4,3,128,2048]{3,2,1,0:T(8,128)(2,1)} custom-call(bf16[2048,2048]{1,0:T(8,128)(2,1)} %virtual_order.1.refs_0_.virt_ref, bf16[3,512,512]{2,1,0:T(8,128)(2,1)S(1)} %get-tuple-element.43.refs_0_.refs_4_, bf16[3,512,512]{2,1,0:T(8,128)(2,1)S(1)} %collective-permute-done.14.refs_1_, ...), custom_call_target="tpu_custom_call" | custom-call | flops 12884901888 | bytes 20971520 | tf_op jit(solution)/shard_map/fully_transformed/pallas_call | solution.py:348
  633.3 34.1 %all-to-all-done.2.returned_ref = bf16[4,5,128,2048]{3,2,1,0:T(8,128)(2,1)} async-done(((bf16[4,5,128,2048]{3,2,1,0:T(8,128)(2,1)}), bf16[4,5,128,2048]{3,2,1,0:T(8,128)(2,1)}, u32[]{:S(2)}, u32[]{:S(2)}) %all-to-all-start.2) | async-done | bytes 10485792 | tf_op jit(solution)/shard_map/all_to_all | solution.py:382
  681.1 89.6 %collective-permute-done.17.refs_0_.refs_3_ = bf16[32,128,512]{2,1,0:T(8,128)(2,1)} collective-permute-done((bf16[32,128,512]{2,1,0:T(8,128)(2,1)S(1)}, bf16[32,128,512]{2,1,0:T(8,128)(2,1)}, u32[]{:S(2)}, u32[]{:S(2)}) %collective-permute-start.17) | collective-permute-done | bytes 4194336 | tf_op jit(solution)/shard_map/ppermute | solution.py:21
  770.7 17.5 %contracted.3 = f32[2,32,320]{2,1,0:T(8,128)S(1)} custom-call(bf16[4,5,128,2048]{3,2,1,0:T(8,128)(2,1)} %all-to-all-done.2.returned_ref, bf16[32,128,512]{2,1,0:T(8,128)(2,1)} %get-tuple-element.40.refs_0_, bf16[32,128,512]{2,1,0:T(8,128)(2,1)} %collective-permute-done.9.refs_5_.refs_1_, bf16[32,128,512]{2,1,0:T(8,128)(2,1)} %collective-permute-done.10.refs_6_.refs_2_, ...), custom_call_target="tpu_custom_call" | custom-call | flops 8053063680 | bytes 33030144 | tf_op jit(solution)/shard_map/contracted/pallas_call | solution.py:259
  791.2 7.5 contracted.4
  819.5 14.1 %contracted.5 = f32[2,32,192]{2,1,0:T(8,128)S(1)} custom-call(bf16[4,3,128,2048]{3,2,1,0:T(8,128)(2,1)} %all-to-all-done.4.returned_ref, bf16[32,128,512]{2,1,0:T(8,128)(2,1)S(1)} %copy-done.4, bf16[32,128,512]{2,1,0:T(8,128)(2,1)S(1)} %copy-done.6, bf16[32,128,512]{2,1,0:T(8,128)(2,1)S(1)} %copy-done.8, bf16[32,128,512]{2,1,0:T(8,128)(2,1)} %copy-done.9, ...), custom_call_target="tpu_custom_call" | custom-call | flops 6442450944 | bytes 39845888 | tf_op jit(solution)/shard_map/contracted/pallas_call | solution.py:259
  834.3 14.4 %all_to_all.30 = f32[16,1,2048]{2,1,0:T(1,128)S(1)} all-to-all(f32[16,1,2048]{2,1,0:T(1,128)S(1)} %reshape.27), channel_id=1, replica_groups=mesh['aux'=2,'row'=4,'col'=4] {'row','col'}, dimensions={0} | all-to-all | bytes 262144 | tf_op jit(solution)/shard_map/all_to_all | solution.py:443
  (90 shorter events, 95.7 us)
Async XLA Ops:
  6.5 90.7 %all-gather.5.cloned.1.call-start = ((), (), s32[]{:S(2)}) async-start(), calls=%async_computation.6 | async-start | bytes 2621440 | tf_op jit(solution)/shard_map/all_gather | solution.py:399
  13.2 88.2 %all-to-all-start = ((bf16[4,1,512,512]{3,2,1,0:T(8,128)(2,1)}), bf16[4,1,512,512]{3,2,1,0:T(8,128)(2,1)S(1)}, u32[]{:S(2)}, u32[]{:S(2)}) async-start(bf16[4,1,512,512]{3,2,1,0:T(8,128)(2,1)} %masked_piece.3.refs_2_.refs_0_), calls=%async_computation | async-start | bytes 4194304 | tf_op jit(solution)/shard_map/all_to_all | solution.py:382
  19.5 172.4 %all-gather.7.cloned.1.call-start = ((), (), s32[]{:S(2)}) async-start(), calls=%async_computation.7 | async-start | bytes 18874368 | tf_op jit(solution)/shard_map/all_gather | solution.py:401
  102.8 188.2 %all-to-all-start.1 = ((bf16[4,4,512,512]{3,2,1,0:T(8,128)(2,1)}), bf16[4,4,512,512]{3,2,1,0:T(8,128)(2,1)}, u32[]{:S(2)}, u32[]{:S(2)}) async-start(bf16[4,4,512,512]{3,2,1,0:T(8,128)(2,1)} %masked_piece.4.refs_2_.refs_0_), calls=%async_computation.1 | async-start | bytes 16777216 | tf_op jit(solution)/shard_map/all_to_all | solution.py:382
  206.2 12.7 %copy-start.2 = (bf16[4,1,512,512]{3,2,1,0:T(8,128)(2,1)S(1)}, bf16[4,1,512,512]{3,2,1,0:T(8,128)(2,1)}, u32[]{:S(2)}) copy-start(bf16[4,1,512,512]{3,2,1,0:T(8,128)(2,1)} %copy-done.1) | copy-start | bytes 6291460
  227.9 14.8 %collective-permute-start = (bf16[1,512,512]{2,1,0:T(8,128)(2,1)S(1)}, bf16[1,512,512]{2,1,0:T(8,128)(2,1)S(1)}, u32[]{:S(2)}, u32[]{:S(2)}) collective-permute-start(bf16[1,512,512]{2,1,0:T(8,128)(2,1)S(1)} %get-tuple-element.29), channel_id=1, source_target_pairs={{0,1},{1,0},{2,3},{3,2},{4,5},{5,4},{6,7},{7,6},{8,9},{9,8},{10,11... | collective-permute-start | bytes 1572872 | tf_op jit(solution)/shard_map/ppermute | solution.py:21
  229.4 25.0 %collective-permute-start.1 = (bf16[1,512,512]{2,1,0:T(8,128)(2,1)S(1)}, bf16[1,512,512]{2,1,0:T(8,128)(2,1)S(1)}, u32[]{:S(2)}, u32[]{:S(2)}) collective-permute-start(bf16[1,512,512]{2,1,0:T(8,128)(2,1)S(1)} %get-tuple-element.30), channel_id=1, source_target_pairs={{0,2},{1,3},{2,0},{3,1},{4,6},{5,7},{6,4},{7,5},{8,10},{9,11},{10,... | collective-permute-start | bytes 1572872 | tf_op jit(solution)/shard_map/ppermute | solution.py:21
  230.0 24.5 %collective-permute-start.2 = (bf16[1,512,512]{2,1,0:T(8,128)(2,1)S(1)}, bf16[1,512,512]{2,1,0:T(8,128)(2,1)S(1)}, u32[]{:S(2)}, u32[]{:S(2)}) collective-permute-start(bf16[1,512,512]{2,1,0:T(8,128)(2,1)S(1)} %get-tuple-element.31), channel_id=1, source_target_pairs={{0,3},{1,2},{2,1},{3,0},{4,7},{5,6},{6,5},{7,4},{8,11},{9,10},{10,... | collective-permute-start | bytes 1572872 | tf_op jit(solution)/shard_map/ppermute | solution.py:21
  291.0 142.9 %all-to-all-start.3 = ((bf16[4,3,512,512]{3,2,1,0:T(8,128)(2,1)}), bf16[4,3,512,512]{3,2,1,0:T(8,128)(2,1)}, u32[]{:S(2)}, u32[]{:S(2)}) async-start(bf16[4,3,512,512]{3,2,1,0:T(8,128)(2,1)} %ordered.3.refs_0_), calls=%async_computation.3 | async-start | bytes 12582912 | tf_op jit(solution)/shard_map/all_to_all | solution.py:382
  311.4 26.2 %collective-permute-start.6 = (bf16[2,512,512]{2,1,0:T(8,128)(2,1)S(1)}, bf16[2,512,512]{2,1,0:T(8,128)(2,1)S(1)}, u32[]{:S(2)}, u32[]{:S(2)}) collective-permute-start(bf16[2,512,512]{2,1,0:T(8,128)(2,1)S(1)} %get-tuple-element.37), channel_id=1, source_target_pairs={{0,1},{1,0},{2,3},{3,2},{4,5},{5,4},{6,7},{7,6},{8,9},{9,8},{10,11... | collective-permute-start | bytes 3145736 | tf_op jit(solution)/shard_map/ppermute | solution.py:21
  313.0 48.6 %collective-permute-start.7 = (bf16[2,512,512]{2,1,0:T(8,128)(2,1)S(1)}, bf16[2,512,512]{2,1,0:T(8,128)(2,1)S(1)}, u32[]{:S(2)}, u32[]{:S(2)}) collective-permute-start(bf16[2,512,512]{2,1,0:T(8,128)(2,1)S(1)} %get-tuple-element.38), channel_id=1, source_target_pairs={{0,2},{1,3},{2,0},{3,1},{4,6},{5,7},{6,4},{7,5},{8,10},{9,11},{10,... | collective-permute-start | bytes 3145736 | tf_op jit(solution)/shard_map/ppermute | solution.py:21
  314.5 47.0 %collective-permute-start.8 = (bf16[2,512,512]{2,1,0:T(8,128)(2,1)S(1)}, bf16[2,512,512]{2,1,0:T(8,128)(2,1)S(1)}, u32[]{:S(2)}, u32[]{:S(2)}) collective-permute-start(bf16[2,512,512]{2,1,0:T(8,128)(2,1)S(1)} %get-tuple-element.39), channel_id=1, source_target_pairs={{0,3},{1,2},{2,1},{3,0},{4,7},{5,6},{6,5},{7,4},{8,11},{9,10},{10,... | collective-permute-start | bytes 3145736 | tf_op jit(solution)/shard_map/ppermute | solution.py:21
  329.8 52.7 %collective-permute-start.3 = (bf16[2,512,512]{2,1,0:T(8,128)(2,1)S(1)}, bf16[2,512,512]{2,1,0:T(8,128)(2,1)S(1)}, u32[]{:S(2)}, u32[]{:S(2)}) collective-permute-start(bf16[2,512,512]{2,1,0:T(8,128)(2,1)S(1)} %get-tuple-element.34), channel_id=1, source_target_pairs={{0,1},{1,0},{2,3},{3,2},{4,5},{5,4},{6,7},{7,6},{8,9},{9,8},{10,11... | collective-permute-start | bytes 3145736 | tf_op jit(solution)/shard_map/ppermute | solution.py:21
  331.3 72.9 %collective-permute-start.4 = (bf16[2,512,512]{2,1,0:T(8,128)(2,1)S(1)}, bf16[2,512,512]{2,1,0:T(8,128)(2,1)S(1)}, u32[]{:S(2)}, u32[]{:S(2)}) collective-permute-start(bf16[2,512,512]{2,1,0:T(8,128)(2,1)S(1)} %get-tuple-element.35), channel_id=1, source_target_pairs={{0,2},{1,3},{2,0},{3,1},{4,6},{5,7},{6,4},{7,5},{8,10},{9,11},{10,... | collective-permute-start | bytes 3145736 | tf_op jit(solution)/shard_map/ppermute | solution.py:21
  337.6 66.6 %collective-permute-start.5 = (bf16[2,512,512]{2,1,0:T(8,128)(2,1)S(1)}, bf16[2,512,512]{2,1,0:T(8,128)(2,1)S(1)}, u32[]{:S(2)}, u32[]{:S(2)}) collective-permute-start(bf16[2,512,512]{2,1,0:T(8,128)(2,1)S(1)} %get-tuple-element.36), channel_id=1, source_target_pairs={{0,3},{1,2},{2,1},{3,0},{4,7},{5,6},{6,5},{7,4},{8,11},{9,10},{10,... | collective-permute-start | bytes 3145736 | tf_op jit(solution)/shard_map/ppermute | solution.py:21
  433.9 233.5 %all-to-all-start.2 = ((bf16[4,5,128,2048]{3,2,1,0:T(8,128)(2,1)}), bf16[4,5,128,2048]{3,2,1,0:T(8,128)(2,1)}, u32[]{:S(2)}, u32[]{:S(2)}) async-start(bf16[4,5,128,2048]{3,2,1,0:T(8,128)(2,1)} %fully_transformed.6.refs_3_.refs_0_), calls=%async_computation.2 | async-start | bytes 20971520 | tf_op jit(solution)/shard_map/all_to_all | solution.py:382
  450.8 93.8 %collective-permute-start.10 = (bf16[32,128,512]{2,1,0:T(8,128)(2,1)}, bf16[32,128,512]{2,1,0:T(8,128)(2,1)}, u32[]{:S(2)}, u32[]{:S(2)}) collective-permute-start(bf16[32,128,512]{2,1,0:T(8,128)(2,1)} %get-tuple-element.42), channel_id=1, source_target_pairs={{0,2},{1,3},{2,0},{3,1},{4,6},{5,7},{6,4},{7,5},{8,10},{9,11},{10,... | collective-permute-start | bytes 12582920 | tf_op jit(solution)/shard_map/ppermute | solution.py:21
  452.3 93.8 %collective-permute-start.9 = (bf16[32,128,512]{2,1,0:T(8,128)(2,1)}, bf16[32,128,512]{2,1,0:T(8,128)(2,1)}, u32[]{:S(2)}, u32[]{:S(2)}) collective-permute-start(bf16[32,128,512]{2,1,0:T(8,128)(2,1)} %get-tuple-element.41), channel_id=1, source_target_pairs={{0,1},{1,0},{2,3},{3,2},{4,5},{5,4},{6,7},{7,6},{8,9},{9,8},{10,11... | collective-permute-start | bytes 12582920 | tf_op jit(solution)/shard_map/ppermute | solution.py:21
  474.8 104.9 %collective-permute-start.14 = (bf16[3,512,512]{2,1,0:T(8,128)(2,1)S(1)}, bf16[3,512,512]{2,1,0:T(8,128)(2,1)S(1)}, u32[]{:S(2)}, u32[]{:S(2)}) collective-permute-start(bf16[3,512,512]{2,1,0:T(8,128)(2,1)S(1)} %get-tuple-element.44), channel_id=1, source_target_pairs={{0,1},{1,0},{2,3},{3,2},{4,5},{5,4},{6,7},{7,6},{8,9},{9,8},{10,11... | collective-permute-start | bytes 4718600 | tf_op jit(solution)/shard_map/ppermute | solution.py:21
  475.4 104.3 %collective-permute-start.15 = (bf16[3,512,512]{2,1,0:T(8,128)(2,1)S(1)}, bf16[3,512,512]{2,1,0:T(8,128)(2,1)S(1)}, u32[]{:S(2)}, u32[]{:S(2)}) collective-permute-start(bf16[3,512,512]{2,1,0:T(8,128)(2,1)S(1)} %get-tuple-element.45), channel_id=1, source_target_pairs={{0,2},{1,3},{2,0},{3,1},{4,6},{5,7},{6,4},{7,5},{8,10},{9,11},{10,... | collective-permute-start | bytes 4718600 | tf_op jit(solution)/shard_map/ppermute | solution.py:21
  475.9 135.2 %collective-permute-start.16 = (bf16[3,512,512]{2,1,0:T(8,128)(2,1)}, bf16[3,512,512]{2,1,0:T(8,128)(2,1)S(1)}, u32[]{:S(2)}, u32[]{:S(2)}) collective-permute-start(bf16[3,512,512]{2,1,0:T(8,128)(2,1)} %get-tuple-element.46), channel_id=1, source_target_pairs={{0,3},{1,2},{2,1},{3,0},{4,7},{5,6},{6,5},{7,4},{8,11},{9,10},{10,... | collective-permute-start | bytes 4718600 | tf_op jit(solution)/shard_map/ppermute | solution.py:21
  667.4 145.5 %all-to-all-start.4 = ((bf16[4,3,128,2048]{3,2,1,0:T(8,128)(2,1)}), bf16[4,3,128,2048]{3,2,1,0:T(8,128)(2,1)}, u32[]{:S(2)}, u32[]{:S(2)}) async-start(bf16[4,3,128,2048]{3,2,1,0:T(8,128)(2,1)} %fully_transformed.7.refs_6_.refs_1_.refs_2_.refs_8_), calls=%async_computation.4 | async-start | bytes 12582912 | tf_op jit(solution)/shard_map/all_to_all | solution.py:382
  678.1 92.6 %collective-permute-start.17 = (bf16[32,128,512]{2,1,0:T(8,128)(2,1)S(1)}, bf16[32,128,512]{2,1,0:T(8,128)(2,1)}, u32[]{:S(2)}, u32[]{:S(2)}) collective-permute-start(bf16[32,128,512]{2,1,0:T(8,128)(2,1)S(1)} %masked_strips.3), channel_id=1, source_target_pairs={{0,3},{1,2},{2,1},{3,0},{4,7},{5,6},{6,5},{7,4},{8,11},{9,10},{10,... | collective-permute-start | bytes 12582920 | tf_op jit(solution)/shard_map/ppermute | solution.py:21
  680.6 90.1 %collective-permute-start.11 = (bf16[32,128,512]{2,1,0:T(8,128)(2,1)}, bf16[32,128,512]{2,1,0:T(8,128)(2,1)}, u32[]{:S(2)}, u32[]{:S(2)}) collective-permute-start(bf16[32,128,512]{2,1,0:T(8,128)(2,1)} %get-tuple-element.40.refs_0_), channel_id=1, source_target_pairs={{0,16},{16,0},{1,17},{17,1},{2,18},{18,2},{3,19},{19,3},{4,20},{20... | collective-permute-start | bytes 12582920 | tf_op jit(solution)/shard_map/ppermute | solution.py:21
  680.6 90.1 %collective-permute-start.12 = (bf16[32,128,512]{2,1,0:T(8,128)(2,1)}, bf16[32,128,512]{2,1,0:T(8,128)(2,1)}, u32[]{:S(2)}, u32[]{:S(2)}) collective-permute-start(bf16[32,128,512]{2,1,0:T(8,128)(2,1)} %collective-permute-done.9.refs_5_.refs_1_), channel_id=1, source_target_pairs={{0,16},{16,0},{1,17},{17,1},{2,18},{18,2},{3,19},{19,3},{4,20},{20... | collective-permute-start | bytes 12582920 | tf_op jit(solution)/shard_map/ppermute | solution.py:21
  681.1 89.6 %collective-permute-start.13 = (bf16[32,128,512]{2,1,0:T(8,128)(2,1)}, bf16[32,128,512]{2,1,0:T(8,128)(2,1)}, u32[]{:S(2)}, u32[]{:S(2)}) collective-permute-start(bf16[32,128,512]{2,1,0:T(8,128)(2,1)} %collective-permute-done.10.refs_6_.refs_2_), channel_id=1, source_target_pairs={{0,16},{16,0},{1,17},{17,1},{2,18},{18,2},{3,19},{19,3},{4,20},{20... | collective-permute-start | bytes 12582920 | tf_op jit(solution)/shard_map/ppermute | solution.py:21
  770.7 17.7 %collective-permute-start.18 = (bf16[32,128,512]{2,1,0:T(8,128)(2,1)}, bf16[32,128,512]{2,1,0:T(8,128)(2,1)}, u32[]{:S(2)}, u32[]{:S(2)}) collective-permute-start(bf16[32,128,512]{2,1,0:T(8,128)(2,1)} %collective-permute-done.17.refs_0_.refs_3_), channel_id=1, source_target_pairs={{0,16},{16,0},{1,17},{17,1},{2,18},{18,2},{3,19},{19,3},{4,20},{20... | collective-permute-start | bytes 12582920 | tf_op jit(solution)/shard_map/ppermute | solution.py:21
  788.4 2.8 copy-start
  808.8 2.1 copy-start.7
  812.9 2.2 copy-start.4
  815.1 2.2 copy-start.6
  817.3 2.2 copy-start.8
  (5 other events, 8.5 us)
Sparse Core Ops, SparseCore 0:
  13.3 83.8 all-gather.4
  102.9 88.9 all-gather.6
